TPU v7x, 32 devices: a whole 2x2x4 slice. The times are simulated.
32 devices in a mesh: dp: 4 (over x, core), tm: 4 (over z), space: 2 (over y).
Axes of the slice: x: 2, y: 2, z: 4, core: 2. Of those that a mesh axis runs over, the one named last changes fastest.
Arguments:
- feats: bfloat16 [4, 4, 16, 128, 256], P('dp', 'tm', 'space'), may hold values from -6 to 6
- w_spatial: bfloat16 [3, 3, 256, 256], replicated, may hold values from -0.125 to 0.125
- w_temporal: bfloat16 [768, 256], replicated, may hold values from -0.21875 to 0.21875
- teacher_mid: bfloat16 [4, 4, 16, 128, 256], P('dp', 'tm', 'space'), may hold values from -6 to 6
- w_down: bfloat16 [2, 2, 256, 512], replicated, may hold values from -0.1875 to 0.1875
- w_query: bfloat16 [512, 512], replicated, may hold values from -8 to 8
- w_key: bfloat16 [512, 512], replicated, may hold values from -1 to 1
- w_value: bfloat16 [512, 512], replicated, may hold values from -0.25 to 0.25
- w_out: bfloat16 [512, 512], replicated, may hold values from -0.25 to 0.25
- teacher_top: bfloat16 [4, 4, 8, 64, 512], P('dp', 'tm', 'space'), may hold values from -6 to 6
Outputs:
- student_top: bfloat16 [4, 4, 8, 64, 512], P('dp', 'tm', 'space')
- grad_temporal: float32 [768, 256], P(('tm', 'space'))
- grad_out: float32 [512, 512], P(('tm', 'space'))
All inputs are finite; a program needn't handle non-finite values.
Results may differ from a plain program's by a relative error of at most 0.0075.
Values may be sent and summed in bfloat16 or wider, within the bound.
A program may use at most 64 MiB of HBM per device.

v0:
```python
import math

import jax
import jax.numpy as jnp
from jax import lax
from jax.sharding import PartitionSpec as P


def extended(cells, sides, width):
    for axis, dim in sides:
        count = lax.axis_size(axis)
        ends = count - 1
        head = lax.slice_in_dim(cells, 0, width, axis=dim)
        tail = lax.slice_in_dim(cells, cells.shape[dim] - width, cells.shape[dim], axis=dim)
        cells = jnp.concatenate(
            [
                lax.ppermute(tail, axis, [(i, (i + 1) % count) for i in range(ends)]),
                cells,
                lax.ppermute(head, axis, [((i + 1) % count, i) for i in range(ends)]),
            ],
            axis=dim,
        )
    return cells


def from_behind(block, axis, distance):
    devices = range(lax.axis_size(axis))
    route = [(i - distance, i) for i in devices if i - distance in devices]
    return lax.ppermute(block, axis, route)


def local(
    feats, w_spatial, w_temporal, teacher_mid, w_down, w_query, w_key, w_value, w_out, teacher_top
):
    numbers = ("NHWC", "HWIO", "NHWC")
    frame_in = feats[0, 0]
    rows_here, cols_here, chan = frame_in.shape
    devices_all = lax.axis_size("dp") * lax.axis_size("tm") * lax.axis_size("space")
    group = lax.axis_size("tm") * lax.axis_size("space")
    padded = extended(frame_in, (("space", 0),), 1)
    conv = lax.conv_general_dilated(
        padded[None],
        w_spatial,
        (1, 1),
        ((0, 0), (1, 1)),
        dimension_numbers=numbers,
        preferred_element_type=jnp.float32,
    )[0]
    spatial = jax.nn.silu(conv).astype(jnp.bfloat16)
    back_one = from_behind(spatial, "tm", 1)
    back_two = from_behind(spatial, "tm", 2)
    stacked = jnp.concatenate([back_two, back_one, spatial], -1).reshape(
        rows_here * cols_here, 3 * chan
    )
    temporal = jnp.dot(stacked, w_temporal, preferred_element_type=jnp.float32)
    mid = (frame_in.reshape(-1, chan).astype(jnp.float32) + temporal).astype(jnp.bfloat16)
    diff_mid = (
        mid.astype(jnp.float32) - teacher_mid[0, 0].reshape(-1, chan).astype(jnp.float32)
    ).astype(jnp.bfloat16)
    scale_mid = 1.0 / math.sqrt(rows_here * cols_here * devices_all)
    columns = stacked
    share_temporal = lax.psum_scatter(
        lax.dot_general(
            columns, diff_mid, (((0,), (0,)), ((), ())), preferred_element_type=jnp.float32
        )
        * scale_mid,
        ("tm", "space"),
        scatter_dimension=0,
        tiled=True,
    )
    coarse = lax.conv_general_dilated(
        mid.reshape(1, rows_here, cols_here, chan),
        w_down,
        (2, 2),
        "VALID",
        dimension_numbers=numbers,
        preferred_element_type=jnp.float32,
    )[0].astype(jnp.bfloat16)
    half_rows, half_cols, width = coarse.shape
    points = half_rows * half_cols
    coarse = coarse.reshape(points, width)
    score_scale = 1.0 / math.sqrt(width)
    frames_all = lax.axis_size("tm")
    share_points = points // frames_all
    piece = lax.all_to_all(
        coarse.reshape(1, frames_all, share_points, width),
        "tm",
        split_axis=1,
        concat_axis=0,
        tiled=True,
    )
    frame_count = piece.shape[0]
    count = piece.shape[2]
    rows_in = piece.reshape(frame_count * count, width)
    query = jnp.dot(rows_in, w_query, preferred_element_type=jnp.float32).astype(jnp.bfloat16)
    key = jnp.dot(rows_in, w_key, preferred_element_type=jnp.float32).astype(jnp.bfloat16)
    value = jnp.dot(rows_in, w_value, preferred_element_type=jnp.float32).astype(jnp.bfloat16)
    query, key, value = (query, key, value)
    query_f = query.astype(jnp.float32).reshape(frame_count, count, width)
    key_f = key.astype(jnp.float32).reshape(frame_count, count, width)
    value_f = value.astype(jnp.float32).reshape(frame_count, count, width)
    scores = jnp.einsum("qpd,kpd->pqk", query_f, key_f) * score_scale
    later = jnp.arange(frame_count)[:, None] >= jnp.arange(frame_count)[None, :]
    scores = jnp.where(later[None], scores, -jnp.inf)
    top_score = jnp.max(scores, -1, keepdims=True)
    weights = jnp.exp(scores - top_score)
    totals = jnp.sum(weights, -1)
    result = jnp.einsum("pqk,kpd->qpd", weights, value_f) / jnp.transpose(totals, (1, 0))[..., None]
    result = result.astype(jnp.bfloat16).reshape(frame_count, 1, count, width)
    moved = lax.all_to_all(result, "tm", split_axis=0, concat_axis=1, tiled=True)
    attended = moved.reshape(points, width)
    out = jnp.dot(attended, w_out, preferred_element_type=jnp.float32)
    student = (coarse.astype(jnp.float32) + out).astype(jnp.bfloat16)
    diff_top = (
        student.astype(jnp.float32) - teacher_top[0, 0].reshape(points, width).astype(jnp.float32)
    ).astype(jnp.bfloat16)
    scale_top = 1.0 / math.sqrt(points * devices_all)
    columns = lax.slice_in_dim(
        attended, 0, lax.axis_size(("tm", "space")) * (width // group), axis=1
    )
    share_out = lax.psum_scatter(
        lax.dot_general(
            columns, diff_top, (((0,), (0,)), ((), ())), preferred_element_type=jnp.float32
        )
        * scale_top,
        ("tm", "space"),
        scatter_dimension=0,
        tiled=True,
    )
    grad_temporal, grad_out = lax.psum((share_temporal, share_out), "dp")
    return (student.reshape(1, 1, half_rows, half_cols, width), grad_temporal, grad_out)


def solution(mesh):
    return jax.shard_map(
        local,
        mesh=mesh,
        in_specs=(
            P("dp", "tm", "space", None, None),
            P(),
            P(),
            P("dp", "tm", "space", None, None),
            P(),
            P(),
            P(),
            P(),
            P(),
            P("dp", "tm", "space", None, None),
        ),
        out_specs=(
            P("dp", "tm", "space", None, None),
            P(("tm", "space"), None),
            P(("tm", "space"), None),
        ),
        check_vma=False,
    )
```

profile of v0, /device:TPU:0, one launch (start us, length us, event | category | flops | bytes accessed | tf_op | source)
XLA Modules:
  0.0 244.7 jit_solution(15843467934365717020)
XLA Ops:
  7.2 0.0 copy-start
  7.2 1.0 slice_bitcast_fusion.2
  8.2 4.9 %collective-permute-start = (bf16[1,128,256]{2,1,0:T(8,128)(2,1)S(1)}, bf16[1,128,256]{2,1,0:T(8,128)(2,1)S(1)}, u32[]{:S(2)}, u32[]{:S(2)}) collective-permute-start(bf16[1,128,256]{2,1,0:T(8,128)(2,1)S(1)} %get-tuple-element.5), channel_id=1, source_target_pairs={{0,1},{2,3},{4,5},{6,7},{8,9},{10,11},{12,13},{14,15},{16,17},{18,... | collective-permute-start | bytes 196616 | tf_op jit(solution)/shard_map/ppermute | solution.py:17
  13.0 1.3 collective-permute-start.1
  14.3 0.6 collective-permute-done
  14.9 4.3 %collective-permute-done.1 = bf16[1,128,256]{2,1,0:T(8,128)(2,1)S(1)} collective-permute-done((bf16[1,128,256]{2,1,0:T(8,128)(2,1)S(1)}, bf16[1,128,256]{2,1,0:T(8,128)(2,1)S(1)}, u32[]{:S(2)}, u32[]{:S(2)}) %collective-permute-start.1) | collective-permute-done | bytes 65568 | tf_op jit(solution)/shard_map/ppermute | solution.py:19
  19.2 1.1 maximum_bitcast_fusion
  20.3 0.2 pad
  20.5 0.0 copy-start.11
  20.5 0.2 reshape.79
  20.8 0.1 copy.43
  20.9 0.0 copy-done
  21.0 0.2 copy-done.11
  21.2 1.5 convolution_select_fusion
  22.7 0.4 copy.44
  23.0 0.3 multiply_convert_fusion
  23.3 3.5 %collective-permute-start.3 = (bf16[8,128,256]{2,0,1:T(8,128)(2,1)S(1)}, bf16[8,128,256]{2,0,1:T(8,128)(2,1)S(1)}, u32[]{:S(2)}, u32[]{:S(2)}) collective-permute-start(bf16[8,128,256]{2,0,1:T(8,128)(2,1)S(1)} %multiply_convert_fusion), channel_id=1, source_target_pairs={{0,2},{2,4},{4,6},{1,3},{3,5},{5,7},{8,10},{10,12},{12,14},{9,11},... | collective-permute-start | bytes 1572872 | tf_op jit(solution)/shard_map/ppermute | solution.py:29
  26.9 4.5 %collective-permute-start.2 = (bf16[8,128,256]{2,0,1:T(8,128)(2,1)S(1)}, bf16[8,128,256]{2,0,1:T(8,128)(2,1)S(1)}, u32[]{:S(2)}, u32[]{:S(2)}) collective-permute-start(bf16[8,128,256]{2,0,1:T(8,128)(2,1)S(1)} %multiply_convert_fusion), channel_id=1, source_target_pairs={{0,4},{2,6},{1,5},{3,7},{8,12},{10,14},{9,13},{11,15},{16,20},{18,... | collective-permute-start | bytes 1572872 | tf_op jit(solution)/shard_map/ppermute | solution.py:29
  31.4 7.8 %collective-permute-done.3 = bf16[8,128,256]{2,0,1:T(8,128)(2,1)S(1)} collective-permute-done((bf16[8,128,256]{2,0,1:T(8,128)(2,1)S(1)}, bf16[8,128,256]{2,0,1:T(8,128)(2,1)S(1)}, u32[]{:S(2)}, u32[]{:S(2)}) %collective-permute-start.3) | collective-permute-done | bytes 524320 | tf_op jit(solution)/shard_map/ppermute | solution.py:29
  39.2 8.7 %collective-permute-done.2 = bf16[8,128,256]{2,0,1:T(8,128)(2,1)S(1)} collective-permute-done((bf16[8,128,256]{2,0,1:T(8,128)(2,1)S(1)}, bf16[8,128,256]{2,0,1:T(8,128)(2,1)S(1)}, u32[]{:S(2)}, u32[]{:S(2)}) %collective-permute-start.2) | collective-permute-done | bytes 524320 | tf_op jit(solution)/shard_map/ppermute | solution.py:29
  47.8 0.1 pad_maximum_fusion
  47.9 0.0 copy-start.2
  48.0 0.0 copy-start.10
  48.0 0.3 copy.45
  48.3 0.7 copy-done.2
  49.0 0.1 copy-done.10
  49.1 0.6 fusion.1
  49.7 0.0 copy-start.7
  49.7 0.2 copy.47
  49.9 0.4 copy-done.9
  50.3 0.4 convolution_convert_fusion.3
  50.8 0.0 copy-done.7
  50.8 0.8 copy.68
  51.6 16.9 %all-to-all-start = ((bf16[1,4,64,512]{3,2,0,1:T(8,128)(2,1)}), bf16[1,4,64,512]{3,2,0,1:T(8,128)(2,1)S(1)}, u32[]{:S(2)}, u32[]{:S(2)}) async-start(bf16[1,4,64,512]{3,2,0,1:T(8,128)(2,1)} %bitcast.51.clone.2), calls=%async_computation | async-start | bytes 524288 | tf_op jit(solution)/shard_map/all_to_all | solution.py:85
  68.4 0.0 reduce-scatter.3.cloned.1.call-start
  68.4 0.0 copy-start.3
  68.4 2.8 %convolution_multiply_fusion.1 = f32[768,256]{1,0:T(8,128)} fusion(bf16[1024,768]{1,0:T(8,128)(2,1)S(1)} %bitcast.75, bf16[1024,256]{1,0:T(8,128)(2,1)} %bitcast.85, bf16[1024,256]{1,0:T(8,128)(2,1)} %copy-done.7), kind=kOutput, calls=%fused_computation.7 | convolution fusion | flops 403898368 | bytes 3407872 | tf_op jit(solution)/shard_map/dot_general | solution.py:63
  71.2 0.0 reduce-scatter.3.cloned.1.call-update
  71.3 0.0 reduce-scatter.5.cloned.1.call-start
  71.3 3.9 %all-to-all-done = bf16[1,4,64,512]{3,2,0,1:T(8,128)(2,1)S(1)} async-done(((bf16[1,4,64,512]{3,2,0,1:T(8,128)(2,1)}), bf16[1,4,64,512]{3,2,0,1:T(8,128)(2,1)S(1)}, u32[]{:S(2)}, u32[]{:S(2)}) %all-to-all-start) | async-done | bytes 262176 | tf_op jit(solution)/shard_map/all_to_all | solution.py:85
  75.2 0.0 copy-done.3
  75.2 0.3 convolution_convert_fusion
  75.5 0.0 copy-start.5
  75.5 0.3 convolution_convert_fusion.1
  75.8 0.5 fusion.38
  76.3 0.1 fusion.29
  76.4 0.1 copy-done.5
  76.5 0.3 convolution_convert_fusion.2
  76.8 0.0 copy-start.6
  76.9 0.4 fusion.5
  77.2 0.0 copy-start.8
  77.3 11.2 %all_to_all.8 = bf16[4,1,64,512]{3,2,1,0:T(8,128)(2,1)S(1)} all-to-all(bf16[4,1,64,512]{3,2,1,0:T(8,128)(2,1)S(1)} %copy.54), channel_id=1, replica_groups=mesh['dp'=4,'tm'=4,'space'=2] {'tm'}, dimensions={0} | all-to-all | bytes 524288 | tf_op jit(solution)/shard_map/all_to_all | solution.py:110
  88.5 1.2 fusion.3
  89.8 0.0 copy-start.1
  89.8 0.0 copy-done.8
  89.8 1.3 convolution_multiply_fusion
  91.1 0.0 reduce-scatter.5.cloned.1.call-update
  91.2 0.0 all-reduce.3.cloned.1.call-start
  91.2 44.4 %reduce-scatter.3.cloned.1.call-done = f32[96,256]{1,0:T(8,128)} async-done(((f32[768,256]{1,0:T(8,128)}), f32[96,256]{1,0:T(8,128)}) %reduce-scatter.3.cloned.1.call-update) | async-done | bytes 98320 | tf_op jit(solution)/shard_map/reduce_scatter | solution.py:62
  135.6 66.1 %reduce-scatter.5.cloned.1.call-done = f32[64,512]{1,0:T(8,128)} async-done(((f32[512,512]{1,0:T(8,128)}), f32[64,512]{1,0:T(8,128)}) %reduce-scatter.5.cloned.1.call-update) | async-done | bytes 131088 | tf_op jit(solution)/shard_map/reduce_scatter | solution.py:121
  201.7 0.0 all-reduce.3.cloned.1.call-update
  201.7 33.3 %all-reduce.3.cloned.1.call-done = (f32[96,256]{1,0:T(8,128)}, f32[64,512]{1,0:T(8,128)}) async-done(((f32[96,256]{1,0:T(8,128)}, f32[64,512]{1,0:T(8,128)}), (f32[96,256]{1,0:T(8,128)}, f32[64,512]{1,0:T(8,128)})) %all-reduce.3.cloned.1.call-update) | async-done | bytes 229392 | tf_op jit(solution)/shard_map/psum | solution.py:130
  235.1 1.5 copy.71
  236.6 1.6 copy.72
  (9 shorter events, 0.1 us)
Async XLA Ops:
  7.2 13.8 %copy-start = (bf16[3,3,256,256]{3,2,1,0:T(8,128)(2,1)S(1)}, bf16[3,3,256,256]{3,2,1,0:T(8,128)(2,1)}, u32[]{:S(2)}) copy-start(bf16[3,3,256,256]{3,2,1,0:T(8,128)(2,1)} %param.11) | copy-start | bytes 3538948
  8.2 6.8 %collective-permute-start = (bf16[1,128,256]{2,1,0:T(8,128)(2,1)S(1)}, bf16[1,128,256]{2,1,0:T(8,128)(2,1)S(1)}, u32[]{:S(2)}, u32[]{:S(2)}) collective-permute-start(bf16[1,128,256]{2,1,0:T(8,128)(2,1)S(1)} %get-tuple-element.5), channel_id=1, source_target_pairs={{0,1},{2,3},{4,5},{6,7},{8,9},{10,11},{12,13},{14,15},{16,17},{18,... | collective-permute-start | bytes 196616 | tf_op jit(solution)/shard_map/ppermute | solution.py:17
  13.0 6.2 %collective-permute-start.1 = (bf16[1,128,256]{2,1,0:T(8,128)(2,1)S(1)}, bf16[1,128,256]{2,1,0:T(8,128)(2,1)S(1)}, u32[]{:S(2)}, u32[]{:S(2)}) collective-permute-start(bf16[1,128,256]{2,1,0:T(8,128)(2,1)S(1)} %get-tuple-element.6), channel_id=1, source_target_pairs={{1,0},{3,2},{5,4},{7,6},{9,8},{11,10},{13,12},{15,14},{17,16},{19,... | collective-permute-start | bytes 196616 | tf_op jit(solution)/shard_map/ppermute | solution.py:19
  20.5 0.7 copy-start.11
  23.3 15.9 %collective-permute-start.3 = (bf16[8,128,256]{2,0,1:T(8,128)(2,1)S(1)}, bf16[8,128,256]{2,0,1:T(8,128)(2,1)S(1)}, u32[]{:S(2)}, u32[]{:S(2)}) collective-permute-start(bf16[8,128,256]{2,0,1:T(8,128)(2,1)S(1)} %multiply_convert_fusion), channel_id=1, source_target_pairs={{0,2},{2,4},{4,6},{1,3},{3,5},{5,7},{8,10},{10,12},{12,14},{9,11},... | collective-permute-start | bytes 1572872 | tf_op jit(solution)/shard_map/ppermute | solution.py:29
  26.9 21.0 %collective-permute-start.2 = (bf16[8,128,256]{2,0,1:T(8,128)(2,1)S(1)}, bf16[8,128,256]{2,0,1:T(8,128)(2,1)S(1)}, u32[]{:S(2)}, u32[]{:S(2)}) collective-permute-start(bf16[8,128,256]{2,0,1:T(8,128)(2,1)S(1)} %multiply_convert_fusion), channel_id=1, source_target_pairs={{0,4},{2,6},{1,5},{3,7},{8,12},{10,14},{9,13},{11,15},{16,20},{18,... | collective-permute-start | bytes 1572872 | tf_op jit(solution)/shard_map/ppermute | solution.py:29
  47.9 1.0 copy-start.2
  48.0 1.1 copy-start.10
  49.1 1.2 copy-start.9
  49.7 1.1 copy-start.7
  51.6 23.6 %all-to-all-start = ((bf16[1,4,64,512]{3,2,0,1:T(8,128)(2,1)}), bf16[1,4,64,512]{3,2,0,1:T(8,128)(2,1)S(1)}, u32[]{:S(2)}, u32[]{:S(2)}) async-start(bf16[1,4,64,512]{3,2,0,1:T(8,128)(2,1)} %bitcast.51.clone.2), calls=%async_computation | async-start | bytes 524288 | tf_op jit(solution)/shard_map/all_to_all | solution.py:85
  68.4 67.2 %reduce-scatter.3.cloned.1.call-start = ((), (), s32[]{:S(2)}) async-start(), calls=%async_computation.4 | async-start | bytes 884736 | tf_op jit(solution)/shard_map/reduce_scatter | solution.py:62
  68.4 6.8 %copy-start.3 = (bf16[512,512]{1,0:T(8,128)(2,1)S(1)}, bf16[512,512]{1,0:T(8,128)(2,1)}, u32[]{:S(2)}) copy-start(bf16[512,512]{1,0:T(8,128)(2,1)} %param.16) | copy-start | bytes 1572868
  71.2 4.3 %copy-start.4 = (bf16[512,512]{1,0:T(8,128)(2,1)S(1)}, bf16[512,512]{1,0:T(8,128)(2,1)}, u32[]{:S(2)}) copy-start(bf16[512,512]{1,0:T(8,128)(2,1)} %param.15) | copy-start | bytes 1572868
  71.3 130.4 %reduce-scatter.5.cloned.1.call-start = ((), (), s32[]{:S(2)}) async-start(), calls=%async_computation.5 | async-start | bytes 1179648 | tf_op jit(solution)/shard_map/reduce_scatter | solution.py:121
  75.5 1.0 copy-start.5
  76.8 11.7 %copy-start.6 = (bf16[512,512]{1,0:T(8,128)(2,1)S(1)}, bf16[512,512]{1,0:T(8,128)(2,1)}, u32[]{:S(2)}) copy-start(bf16[512,512]{1,0:T(8,128)(2,1)} %param.18) | copy-start | bytes 1572868
  77.2 12.6 %copy-start.8 = (bf16[1,1,4,64,512]{4,3,2,1,0:T(8,128)(2,1)S(1)}, bf16[1,1,4,64,512]{4,3,2,1,0:T(8,128)(2,1)}, u32[]{:S(2)}) copy-start(bf16[1,1,4,64,512]{4,3,2,1,0:T(8,128)(2,1)} %param.19) | copy-start | bytes 786436
  89.8 111.9 %copy-start.1 = (bf16[256,512]{1,0:T(8,128)(2,1)}, bf16[256,512]{1,0:T(8,128)(2,1)S(1)}, u32[]{:S(2)}) copy-start(bf16[256,512]{1,0:T(8,128)(2,1)S(1)} %fusion.3) | copy-start | bytes 786436
  91.2 143.9 %all-reduce.3.cloned.1.call-start = ((), (), s32[]{:S(2)}) async-start(), calls=%async_computation.6 | async-start | bytes 458752 | tf_op jit(solution)/shard_map/psum | solution.py:130
Sparse Core Ops, SparseCore 0:
  72.5 63.0 reduce-scatter.2
  139.4 62.2 reduce-scatter.4
  204.1 30.9 all-reduce.2
where the time goes:
time: 245 us
  waiting for transfers between devices  169 us (69%)
  starting transfers between devices  31.1 us (13%)
  between operations  14 us (6%)
  blocking collectives  11.2 us (5%)
  matrix products  9.62 us (4%)
  local copies, waits for them, and re-layouts  7.98 us (3%)
    reduce_scatter x1, waiting for transfers between devices, local(): lax.psum_scatter(lax.dot_general(columns, diff_top, (((0,), (0,)), ((), (...  66.1 us
    reduce_scatter x1, waiting for transfers between devices, local(): lax.psum_scatter(lax.dot_general(columns, diff_mid, (((0,), (0,)), ((), (...  44.4 us
    psum x1, waiting for transfers between devices, local(): grad_temporal, grad_out = lax.psum((share_temporal, share_out), 'dp')  33.3 us
    all_to_all x1, starting transfers between devices, local(): lax.all_to_all(coarse.reshape(1, frames_all, share_points, width), 'tm',...  16.9 us
    ppermute x2, waiting for transfers between devices, from_behind(): return lax.ppermute(block, axis, route)  16.5 us
    all_to_all x1, blocking collectives, local(): lax.all_to_all(result, 'tm', split_axis=0, concat_axis=1, tiled=True)  11.2 us
    ppermute x2, starting transfers between devices, from_behind(): return lax.ppermute(block, axis, route)  8.01 us
  transfers between devices with their start and end apart: 8, of which 8 were waited for; matrix products, arithmetic and copies ran while one was open for 3% of the time, Pallas kernels for 0%

commit v1 on v0

v1 whole, which is shorter than its diff:
```python
import functools
import math

import jax
import jax.numpy as jnp
from jax import lax
from jax.experimental import pallas as pl
from jax.experimental.pallas import tpu as pltpu
from jax.sharding import PartitionSpec as P

MESH = pl.DeviceIdType.MESH
F32 = jnp.float32
BF16 = jnp.bfloat16


def dot(a, b):
    return jnp.dot(a, b, preferred_element_type=F32)


def dot_t(a, b):
    return lax.dot_general(a, b, (((0,), (0,)), ((), ())), preferred_element_type=F32)


def kernel(
    frames, spaces, scale_mid, scale_top,
    feats, w_sp, w_tm, teach, w_dn, w_q, w_k, w_v, w_o, teach_top,
    student_out, gt_out, go_out,
    home, v_sp, v_tm, v_dn, v_q, v_k, v_v, v_o,
    cells, edge_send, edges, edge_near, shifted, spat, teacher, teacher_top, mid32, stu,
    in_sem, own_sem, fs, fr, es, er, ts, tr, ps, pr_, ss, sr, hs, hr,
):
    t = lax.axis_index("tm")
    s = lax.axis_index("space")
    rows, _, wc, chan = feats.shape
    half_rows, _, hc, width = teach_top.shape
    peers = [lax.rem(t + i, frames) for i in range(1, frames)]

    loads = [
        pltpu.make_async_copy(src, dst, in_sem.at[i])
        for i, (src, dst) in enumerate(
            ((feats, home), (w_sp, v_sp), (w_tm, v_tm), (w_dn, v_dn),
             (w_q, v_q), (w_k, v_k), (w_v, v_v), (w_o, v_o))
        )
    ]
    for load in loads:
        load.start()
    own = [
        pltpu.make_async_copy(feats.at[:, t], cells.at[pl.ds(1, rows), t], own_sem.at[0]),
        pltpu.make_async_copy(teach.at[:, t], teacher.at[t], own_sem.at[1]),
        pltpu.make_async_copy(teach_top.at[:, t], teacher_top.at[t], own_sem.at[2]),
    ]
    for copy in own:
        copy.start()

    barrier = pltpu.get_barrier_semaphore()
    for u in peers:
        pl.semaphore_signal(barrier, inc=1, device_id={"tm": u}, device_id_type=MESH)

    @pl.when(s > 0)
    def _():
        pl.semaphore_signal(barrier, inc=1, device_id={"space": s - 1}, device_id_type=MESH)

    @pl.when(s < spaces - 1)
    def _():
        pl.semaphore_signal(barrier, inc=1, device_id={"space": s + 1}, device_id_type=MESH)

    loads[0].wait()
    for u in range(frames):
        if u > 0:
            left = home[:, u - 1, wc - 8:, :].astype(F32)[:, 7, :]
        else:
            left = jnp.zeros((rows, chan), F32)
        if u < frames - 1:
            right = home[:, u + 1, :8, :].astype(F32)[:, 0, :]
        else:
            right = jnp.zeros((rows, chan), F32)
        edge_send[u] = jnp.concatenate([left, right], 0).astype(BF16)

    near = (s > 0).astype(jnp.int32) + (s < spaces - 1).astype(jnp.int32)
    pl.semaphore_wait(barrier, near + (frames - 1))

    def send(src, dst, ssem, rsem, u):
        return pltpu.make_async_remote_copy(
            src_ref=src, dst_ref=dst, send_sem=ssem, recv_sem=rsem,
            device_id={"tm": u}, device_id_type=MESH,
        )

    def feats_copy(u, f):
        return send(home.at[:, u], cells.at[pl.ds(1, rows), f], fs.at[u], fr.at[f], u)

    def edge_copy(u, f):
        return send(edge_send.at[u], edges.at[f], es.at[u], er.at[f], u)

    def teach_copy(u, f):
        return send(teach.at[:, u], teacher.at[f], ts.at[u], tr.at[f], u)

    def top_copy(u, f):
        return send(teach_top.at[:, u], teacher_top.at[f], ps.at[u], pr_.at[f], u)

    def student_copy(u, f):
        return send(stu.at[u], student_out.at[:, f], ss.at[u], sr.at[f], u)

    for u in peers:
        edge_copy(u, t).start()
        feats_copy(u, t).start()
    edges[t] = edge_send[t]
    spat[pl.ds(0, 2)] = jnp.zeros((2,) + spat.shape[1:], BF16)

    @pl.when(s == 0)
    def _():
        cells[0] = jnp.zeros(cells.shape[1:], BF16)
        edge_near[0] = jnp.zeros(edges.shape, BF16)

    @pl.when(s == spaces - 1)
    def _():
        cells[rows + 1] = jnp.zeros(cells.shape[1:], BF16)
        edge_near[1] = jnp.zeros(edges.shape, BF16)

    own[0].wait()
    for f in peers:
        edge_copy(f, f).wait_recv()
        feats_copy(f, f).wait_recv()
    for u in peers:
        teach_copy(u, t).start()
    for u in peers:
        top_copy(u, t).start()

    def halo(src, dst, i, j, to):
        return pltpu.make_async_remote_copy(
            src_ref=src, dst_ref=dst, send_sem=hs.at[i], recv_sem=hr.at[j],
            device_id={"space": to}, device_id_type=MESH,
        )

    def up(to):
        return (halo(cells.at[1], cells.at[rows + 1], 0, 0, to),
                halo(edges, edge_near.at[1], 1, 1, to))

    def down(to):
        return (halo(cells.at[rows], cells.at[0], 2, 2, to),
                halo(edges, edge_near.at[0], 3, 3, to))

    @pl.when(s > 0)
    def _():
        for copy in up(s - 1):
            copy.start()

    @pl.when(s < spaces - 1)
    def _():
        for copy in down(s + 1):
            copy.start()

    column = lax.broadcasted_iota(jnp.int32, (frames, wc, chan), 1)

    def shift(row, left, right):
        x = cells[row].astype(F32)
        a = jnp.where(column == 0, left, pltpu.roll(x, 1, 1))
        b = jnp.where(column == wc - 1, right, pltpu.roll(x, wc - 1, 1))
        flat = (frames * wc, chan)
        shifted[row, :, pl.ds(0, chan)] = a.astype(BF16).reshape(flat)
        shifted[row, :, pl.ds(chan, chan)] = cells[row].reshape(flat)
        shifted[row, :, pl.ds(2 * chan, chan)] = b.astype(BF16).reshape(flat)

    def conv(first, count):
        total = None
        for dy in range(3):
            block = shifted[pl.ds(first + dy, count)].reshape(count * frames * wc, 3 * chan)
            term = dot(block, v_sp[dy])
            total = term if total is None else total + term
        out = (total / (1.0 + jnp.exp(-total))).astype(BF16)
        out = out.reshape(count, frames, wc, chan)
        for i in range(count):
            spat[pl.ds(2, frames), first + i] = out[i]

    side = edges[...].astype(F32)
    for r in range(rows):
        shift(r + 1, side[:, r:r + 1, :], side[:, rows + r:rows + r + 1, :])
    loads[1].wait()
    for first in range(1, rows - 1, 2):
        conv(first, 2)

    @pl.when(s < spaces - 1)
    def _():
        for copy in up(s + 1):
            copy.wait_recv()

    @pl.when(s > 0)
    def _():
        for copy in down(s - 1):
            copy.wait_recv()

    side = edge_near[0].astype(F32)
    shift(0, side[:, rows - 1:rows, :], side[:, 2 * rows - 1:2 * rows, :])
    side = edge_near[1].astype(F32)
    shift(rows + 1, side[:, 0:1, :], side[:, rows:rows + 1, :])
    conv(0, 1)
    conv(rows - 1, 1)

    loads[2].wait()
    half = chan // 2
    for f in range(frames):
        total = None
        for k in range(3):
            term = dot(spat[f + k].reshape(rows * wc, chan), v_tm[pl.ds(k * chan, chan), :])
            total = term if total is None else total + term
        base = cells[pl.ds(1, rows), f].astype(F32).reshape(rows * wc, chan)
        mid = (base + total).astype(BF16).astype(F32)
        for h in range(2):
            mid32[h, pl.ds(f * rows * wc, rows * wc), :] = mid[:, h * half:(h + 1) * half]

    loads[3].wait()
    coarse = None
    count = frames * rows * wc // 2
    for b in range(2):
        part = jnp.concatenate(
            [mid32[h, pl.ds(b, count, stride=2), :] for h in range(2)], -1
        ).reshape(frames * half_rows, 2, hc, chan)
        for a in range(2):
            block = part[:, a].reshape(frames * half_rows * hc, chan).astype(BF16)
            term = dot(block, v_dn[a, b])
            coarse = term if coarse is None else coarse + term
    coarse = coarse.astype(BF16)

    for i in range(4, 8):
        loads[i].wait()
    points = half_rows * hc
    query = dot(coarse, v_q[...]).astype(BF16).astype(F32).reshape(frames, points, width)
    key = dot(coarse, v_k[...]).astype(BF16).astype(F32).reshape(frames, points, width)
    value = dot(coarse, v_v[...]).astype(BF16).astype(F32).reshape(frames, points, width)
    scale = 1.0 / math.sqrt(width)
    results = []
    for q in range(frames):
        score = [jnp.sum(query[q] * key[k], -1, keepdims=True) * scale for k in range(q + 1)]
        top = functools.reduce(jnp.maximum, score)
        weight = [jnp.exp(x - top) for x in score]
        total = functools.reduce(jnp.add, weight)
        acc = functools.reduce(jnp.add, [weight[k] * value[k] for k in range(q + 1)])
        results.append(acc / total)
    attended = jnp.concatenate(results, 0).astype(BF16)
    student = (coarse.astype(F32) + dot(attended, v_o[...])).astype(BF16)
    stu[...] = student.reshape(frames, half_rows, hc, width)
    for u in peers:
        student_copy(u, t).start()
    keep = pltpu.make_async_copy(stu.at[t], student_out.at[:, t], own_sem.at[3])
    keep.start()

    own[1].wait()
    for f in peers:
        teach_copy(f, f).wait_recv()
    n = frames * rows * wc
    mid = jnp.concatenate([mid32[0], mid32[1]], -1)
    diff = (mid - teacher[...].astype(F32).reshape(n, chan)).astype(BF16)
    for k in range(3):
        gt_out[pl.ds(k * chan, chan), :] = (
            dot_t(spat[pl.ds(k, frames)].reshape(n, chan), diff) * scale_mid
        )
    own[2].wait()
    for f in peers:
        top_copy(f, f).wait_recv()
    diff_top = (
        student.astype(F32) - teacher_top[...].astype(F32).reshape(frames * points, width)
    ).astype(BF16)
    go_out[...] = dot_t(attended, diff_top) * scale_top

    keep.wait()
    for u in peers:
        student_copy(u, u).wait_recv()
    for u in peers:
        edge_copy(u, t).wait_send()
        feats_copy(u, t).wait_send()
        teach_copy(u, t).wait_send()
        top_copy(u, t).wait_send()
        student_copy(u, t).wait_send()

    @pl.when(s > 0)
    def _():
        for copy in up(s - 1):
            copy.wait_send()

    @pl.when(s < spaces - 1)
    def _():
        for copy in down(s + 1):
            copy.wait_send()


def local(
    feats, w_spatial, w_temporal, teacher_mid, w_down, w_query, w_key, w_value, w_out, teacher_top
):
    frames = lax.axis_size("tm")
    spaces = lax.axis_size("space")
    devices_all = lax.axis_size("dp") * frames * spaces
    rows, cols, chan = feats.shape[2:]
    half_rows, half_cols, width = teacher_top.shape[2:]
    wc, hc = cols // frames, half_cols // frames
    scale_mid = 1.0 / math.sqrt(rows * cols * devices_all)
    scale_top = 1.0 / math.sqrt(half_rows * half_cols * devices_all)
    dma = pltpu.SemaphoreType.DMA
    student, gt, go = pl.pallas_call(
        functools.partial(kernel, frames, spaces, scale_mid, scale_top),
        out_shape=(
            jax.ShapeDtypeStruct((half_rows, frames, hc, width), BF16),
            jax.ShapeDtypeStruct(w_temporal.shape, F32),
            jax.ShapeDtypeStruct(w_out.shape, F32),
        ),
        in_specs=[pl.BlockSpec(memory_space=pl.ANY)] * 10,
        out_specs=(
            pl.BlockSpec(memory_space=pl.ANY),
            pl.BlockSpec(memory_space=pltpu.VMEM),
            pl.BlockSpec(memory_space=pltpu.VMEM),
        ),
        scratch_shapes=[
            pltpu.VMEM((rows, frames, wc, chan), BF16),
            pltpu.VMEM((3, 3 * chan, chan), BF16),
            pltpu.VMEM(w_temporal.shape, BF16),
            pltpu.VMEM(w_down.shape, BF16),
            pltpu.VMEM(w_query.shape, BF16),
            pltpu.VMEM(w_key.shape, BF16),
            pltpu.VMEM(w_value.shape, BF16),
            pltpu.VMEM(w_out.shape, BF16),
            pltpu.VMEM((rows + 2, frames, wc, chan), BF16),
            pltpu.VMEM((frames, 2 * rows, chan), BF16),
            pltpu.VMEM((frames, 2 * rows, chan), BF16),
            pltpu.VMEM((2, frames, 2 * rows, chan), BF16),
            pltpu.VMEM((rows + 2, frames * wc, 3 * chan), BF16),
            pltpu.VMEM((frames + 2, rows, wc, chan), BF16),
            pltpu.VMEM((frames, rows, wc, chan), BF16),
            pltpu.VMEM((frames, half_rows, hc, width), BF16),
            pltpu.VMEM((2, frames * rows * wc, chan // 2), F32),
            pltpu.VMEM((frames, half_rows, hc, width), BF16),
            dma((8,)),
            dma((4,)),
        ]
        + [dma((frames,))] * 10
        + [dma((4,)), dma((4,))],
        compiler_params=pltpu.CompilerParams(
            collective_id=0, has_side_effects=True, vmem_limit_bytes=40 * 1024 * 1024
        ),
    )(
        feats.reshape(rows, frames, wc, chan),
        w_spatial.reshape(3, 3 * chan, chan),
        w_temporal,
        teacher_mid.reshape(rows, frames, wc, chan),
        w_down,
        w_query,
        w_key,
        w_value,
        w_out,
        teacher_top.reshape(half_rows, frames, hc, width),
    )
    share_t = lax.psum_scatter(gt, ("tm", "space"), scatter_dimension=0, tiled=True)
    share_o = lax.psum_scatter(go, ("tm", "space"), scatter_dimension=0, tiled=True)
    grad_t, grad_o = lax.psum((share_t, share_o), "dp")
    return (student.reshape(1, 1, half_rows, half_cols, width), grad_t, grad_o)


def solution(mesh):
    frame = P("dp", "tm", "space", None, None)
    return jax.shard_map(
        local,
        mesh=mesh,
        in_specs=(frame, P(), P(), frame, P(), P(), P(), P(), P(), frame),
        out_specs=(frame, P(("tm", "space"), None), P(("tm", "space"), None)),
        check_vma=False,
    )
```

time: 245 us -> 235 us (0.959)
  Pallas kernels: 0 us -> 42.3 us
  starting transfers between devices: 31.1 us -> 0.12 us
  blocking collectives: 11.2 us -> 0 us
  matrix products: 9.62 us -> 0 us
  local copies, waits for them, and re-layouts: 7.98 us -> 14.5 us
  waiting for transfers between devices: 169 us -> 164 us
    pallas_call x0 -> x1, Pallas kernels: none -> 42.3 us  [local(): pl.pallas_call(functools.partial(kernel, frames, spaces, scale_mid, scale...]
    ppermute x4 -> x0, waiting for transfers between devices: 21.3 us -> none  [the longest x2 16.5 us: from_behind(): return lax.ppermute(block, axis, route)]
    reduce_scatter x2, waiting for transfers between devices: 110 us -> 130 us  [the longest x1 66.2 us: local(): lax.psum_scatter(go, ('tm', 'space'), scatter_dimension=0, tiled=True)]
    all_to_all x1 -> x0, starting transfers between devices: 16.9 us -> none  [local(): lax.all_to_all(coarse.reshape(1, frames_all, share_points, width), 'tm',...]
    ppermute x4 -> x0, starting transfers between devices: 14.2 us -> none  [the longest x2 8.01 us: from_behind(): return lax.ppermute(block, axis, route)]
    all_to_all x1 -> x0, blocking collectives: 11.2 us -> none  [local(): lax.all_to_all(result, 'tm', split_axis=0, concat_axis=1, tiled=True)]
    unnamed x26 -> x23, local copies, waits for them, and re-layouts: 4.75 us -> 14.5 us
    dot_general x9 -> x0, matrix products: 7.71 us -> none  [the longest x1 2.8 us: local(): lax.dot_general(columns, diff_mid, (((0,), (0,)), ((), ())), preferred_el...]
  transfers between devices with their start and end apart: 8 -> 3, of which waited for: 8 -> 3; matrix products, arithmetic and copies ran while one was open for 3% -> 0% of each run, Pallas kernels for 0% -> 0%
where the time goes in v1:
time: 235 us
  waiting for transfers between devices  164 us (70%)
  Pallas kernels  42.3 us (18%)
  local copies, waits for them, and re-layouts  14.5 us (6%)
  between operations  13.8 us (6%)
    reduce_scatter x1, waiting for transfers between devices, local(): lax.psum_scatter(go, ('tm', 'space'), scatter_dimension=0, tiled=True)  66.2 us
    reduce_scatter x1, waiting for transfers between devices, local(): lax.psum_scatter(gt, ('tm', 'space'), scatter_dimension=0, tiled=True)  63.9 us
    pallas_call x1, Pallas kernels, local(): pl.pallas_call(functools.partial(kernel, frames, spaces, scale_mid, scale...  42.3 us
    psum x1, waiting for transfers between devices, local(): grad_t, grad_o = lax.psum((share_t, share_o), 'dp')  33.4 us
    unnamed x23, local copies, waits for them, and re-layouts  14.5 us
  transfers between devices with their start and end apart: 3, of which 3 were waited for; matrix products, arithmetic and copies ran while one was open for 0% of the time, Pallas kernels for 0%

profile of v1, /device:TPU:0, one launch (start us, length us, event | category | flops | bytes accessed | tf_op | source)
XLA Modules:
  0.0 234.9 jit_solution(6946109087806700591)
XLA Ops:
  7.2 0.0 reduce-scatter.3.cloned.1.call-start
  7.2 0.0 copy-start
  7.2 1.3 copy-done
  8.5 0.0 copy-start.1
  8.5 1.2 copy-done.1
  9.7 0.0 copy-start.2
  9.7 1.0 copy-done.2
  10.8 0.0 copy-start.3
  10.8 1.0 copy-done.3
  11.8 0.0 copy-start.4
  11.8 1.0 copy-done.4
  12.8 0.0 copy-start.5
  12.8 1.0 copy-done.5
  13.9 0.0 copy-start.6
  13.9 1.0 copy-done.6
  14.9 0.0 copy-start.7
  14.9 1.0 copy-done.7
  16.0 0.0 copy-start.8
  16.0 1.0 copy-done.8
  17.0 0.0 copy-start.9
  17.0 0.9 copy-done.9
  17.9 42.3 %shard_map.121 = (bf16[4,4,16,512]{3,2,1,0:T(8,128)(2,1)S(1)}, f32[768,256]{1,0:T(8,128)}, f32[512,512]{1,0:T(8,128)}) custom-call(bf16[8,4,32,256]{3,2,1,0:T(8,128)(2,1)S(1)} %bitcast.6, bf16[3,768,256]{2,1,0:T(8,128)(2,1)S(1)} %bitcast.5, bf16[768,256]{1,0:T(8,128)(2,1)S(1)} %copy-done.8, bf16[8,4,32,256]{3,2,1,0:T(8,128)(2,1)S(1)} %bitcast.7, ...), custom_call_target="tpu_custom_call" | custom-call | tf_op jit(solution)/shard_map/pallas_call | solution.py:297
  60.2 0.0 reduce-scatter.3.cloned.1.call-update
  60.3 0.0 reduce-scatter.5.cloned.1.call-start
  60.3 0.7 reduce-scatter.5.cloned.1.call-update
  61.0 0.0 all-reduce.3.cloned.1.call-start
  61.1 63.9 %reduce-scatter.3.cloned.1.call-done = f32[96,256]{1,0:T(8,128)} async-done(((f32[768,256]{1,0:T(8,128)}), f32[96,256]{1,0:T(8,128)}) %reduce-scatter.3.cloned.1.call-update) | async-done | bytes 98320 | tf_op jit(solution)/shard_map/reduce_scatter | solution.py:349
  125.0 66.2 %reduce-scatter.5.cloned.1.call-done = f32[64,512]{1,0:T(8,128)} async-done(((f32[512,512]{1,0:T(8,128)}), f32[64,512]{1,0:T(8,128)}) %reduce-scatter.5.cloned.1.call-update) | async-done | bytes 131088 | tf_op jit(solution)/shard_map/reduce_scatter | solution.py:350
  191.2 0.0 all-reduce.3.cloned.1.call-update
  191.2 33.4 %all-reduce.3.cloned.1.call-done = (f32[96,256]{1,0:T(8,128)}, f32[64,512]{1,0:T(8,128)}) async-done(((f32[96,256]{1,0:T(8,128)}, f32[64,512]{1,0:T(8,128)}), (f32[96,256]{1,0:T(8,128)}, f32[64,512]{1,0:T(8,128)})) %all-reduce.3.cloned.1.call-update) | async-done | bytes 229392 | tf_op jit(solution)/shard_map/psum | solution.py:351
  224.6 0.7 copy.16
  225.3 1.5 copy.17
  226.8 1.6 copy.18
Async XLA Ops:
  7.2 117.8 %reduce-scatter.3.cloned.1.call-start = ((), (), s32[]{:S(2)}) async-start(), calls=%async_computation.2 | async-start | bytes 884736 | tf_op jit(solution)/shard_map/reduce_scatter | solution.py:349
  7.2 1.3 copy-start
  8.5 1.2 copy-start.1
  9.7 1.0 copy-start.2
  10.8 1.0 copy-start.3
  11.8 1.0 copy-start.4
  12.8 1.0 copy-start.5
  13.9 1.0 copy-start.6
  14.9 1.0 copy-start.7
  16.0 1.0 copy-start.8
  17.0 0.9 copy-start.9
  60.3 130.9 %reduce-scatter.5.cloned.1.call-start = ((), (), s32[]{:S(2)}) async-start(), calls=%async_computation.3 | async-start | bytes 1179648 | tf_op jit(solution)/shard_map/reduce_scatter | solution.py:350
  61.0 163.5 %all-reduce.3.cloned.1.call-start = ((), (), s32[]{:S(2)}) async-start(), calls=%async_computation.4 | async-start | bytes 458752 | tf_op jit(solution)/shard_map/psum | solution.py:351
Sparse Core Ops, SparseCore 0:
  60.4 64.5 reduce-scatter.2
  128.8 62.3 reduce-scatter.4
  193.5 30.9 all-reduce.2

commit v2 on v1

--- a/solution.py
+++ b/solution.py
@@ -21,19 +21,119 @@
     return lax.dot_general(a, b, (((0,), (0,)), ((), ())), preferred_element_type=F32)
 
 
+class Sum:
+    def __init__(self, refs, out, grad, d, me, members, others, spaces):
+        (self.part, self.in1, self.half, self.in2, self.quarter, self.in3, self.done,
+         self.sem12, self.s3, self.r3, self.s4, self.r4) = refs
+        self.out, self.grad, self.d, self.me = out, grad, d, me
+        self.members, self.others, self.spaces = members, others, spaces
+
+    def copy(self, src, dst, ssem, rsem, to):
+        return pltpu.make_async_remote_copy(
+            src_ref=src, dst_ref=dst, send_sem=ssem, recv_sem=rsem,
+            device_id=to, device_id_type=MESH,
+        )
+
+    def one(self):
+        low = lax.rem(self.d, 2)
+        return self.copy(self.part.at[1 - low], self.in1, self.sem12.at[0], self.sem12.at[1],
+                         {"dp": self.d + 1 - 2 * low})
+
+    def two(self):
+        high = self.d // 2
+        return self.copy(self.half.at[1 - high], self.in2, self.sem12.at[2], self.sem12.at[3],
+                         {"dp": self.d + 2 - 4 * high})
+
+    def three(self, g, f):
+        return self.copy(self.quarter.at[g], self.in3.at[f], self.s3.at[g], self.r3.at[f],
+                         {"tm": g // self.spaces, "space": lax.rem(g, self.spaces)})
+
+    def four(self, c, f):
+        return self.copy(self.done.at[f], self.done.at[f], self.s4.at[c], self.r4.at[f],
+                         {"dp": c})
+
+    def first(self):
+        _, group, rows, cols = self.part.shape
+        split = self.grad.astype(BF16).reshape(group, 2, rows, cols)
+        for h in range(2):
+            self.part[h] = split[:, h]
+        self.one().start()
+
+    def second(self):
+        self.one().wait_recv()
+        total = self.part[lax.rem(self.d, 2)].astype(F32) + self.in1[...].astype(F32)
+        cols = self.half.shape[-1]
+        for h in range(2):
+            self.half[h] = total[..., h * cols:(h + 1) * cols].astype(BF16)
+        self.two().start()
+
+    def third(self):
+        self.two().wait_recv()
+        total = self.half[self.d // 2].astype(F32) + self.in2[...].astype(F32)
+        self.quarter[...] = total.astype(BF16)
+        for g in self.members:
+            self.three(g, self.me).start()
+        self.in3[self.me] = self.quarter[self.me]
+
+    def fourth(self):
+        for g in self.members:
+            self.three(g, g).wait_recv()
+        self.done[self.d] = jnp.sum(self.in3[...].astype(F32), 0)
+        for c in self.others:
+            self.four(c, self.d).start()
+
+    def finish(self):
+        for c in self.others:
+            self.four(c, c).wait_recv()
+        count, rows, cols = self.done.shape
+        for c in range(count):
+            self.out[pl.ds((c % 2) * rows, rows), pl.ds((c // 2) * cols, cols)] = self.done[c]
+        self.one().wait_send()
+        self.two().wait_send()
+        for g in self.members:
+            self.three(g, self.me).wait_send()
+        for c in self.others:
+            self.four(c, self.d).wait_send()
+
+
+def sum_scratch(shape, group, clips):
+    dma = pltpu.SemaphoreType.DMA
+    rows, cols = shape[0] // group // 2, shape[1]
+    return [
+        pltpu.VMEM((2, group, rows, cols), BF16),
+        pltpu.VMEM((group, rows, cols), BF16),
+        pltpu.VMEM((2, group, rows, cols // 2), BF16),
+        pltpu.VMEM((group, rows, cols // 2), BF16),
+        pltpu.VMEM((group, rows, cols // 2), BF16),
+        pltpu.VMEM((group, rows, cols // 2), BF16),
+        pltpu.VMEM((clips, rows, cols // 2), F32),
+        dma((4,)),
+        dma((group,)),
+        dma((group,)),
+        dma((clips,)),
+        dma((clips,)),
+    ]
+
+
 def kernel(
-    frames, spaces, scale_mid, scale_top,
+    frames, spaces, clips, reduce, scale_mid, scale_top,
     feats, w_sp, w_tm, teach, w_dn, w_q, w_k, w_v, w_o, teach_top,
     student_out, gt_out, go_out,
     home, v_sp, v_tm, v_dn, v_q, v_k, v_v, v_o,
     cells, edge_send, edges, edge_near, shifted, spat, teacher, teacher_top, mid32, stu,
     in_sem, own_sem, fs, fr, es, er, ts, tr, ps, pr_, ss, sr, hs, hr,
+    *sums,
 ):
     t = lax.axis_index("tm")
     s = lax.axis_index("space")
     rows, _, wc, chan = feats.shape
     half_rows, _, hc, width = teach_top.shape
     peers = [lax.rem(t + i, frames) for i in range(1, frames)]
+    group = frames * spaces
+    me = t * spaces + s
+    members = [lax.rem(me + i, group) for i in range(1, group)]
+    d = lax.axis_index("dp")
+    others = [lax.rem(d + i, clips) for i in range(1, clips)]
 
     loads = [
         pltpu.make_async_copy(src, dst, in_sem.at[i])
@@ -53,16 +153,14 @@
         copy.start()
 
     barrier = pltpu.get_barrier_semaphore()
-    for u in peers:
-        pl.semaphore_signal(barrier, inc=1, device_id={"tm": u}, device_id_type=MESH)
-
-    @pl.when(s > 0)
-    def _():
-        pl.semaphore_signal(barrier, inc=1, device_id={"space": s - 1}, device_id_type=MESH)
-
-    @pl.when(s < spaces - 1)
-    def _():
-        pl.semaphore_signal(barrier, inc=1, device_id={"space": s + 1}, device_id_type=MESH)
+    for g in members:
+        pl.semaphore_signal(
+            barrier, inc=1, device_id={"tm": g // spaces, "space": lax.rem(g, spaces)},
+            device_id_type=MESH,
+        )
+    if reduce:
+        for c in others:
+            pl.semaphore_signal(barrier, inc=1, device_id={"dp": c}, device_id_type=MESH)
 
     loads[0].wait()
     for u in range(frames):
@@ -76,8 +174,7 @@
             right = jnp.zeros((rows, chan), F32)
         edge_send[u] = jnp.concatenate([left, right], 0).astype(BF16)
 
-    near = (s > 0).astype(jnp.int32) + (s < spaces - 1).astype(jnp.int32)
-    pl.semaphore_wait(barrier, near + (frames - 1))
+    pl.semaphore_wait(barrier, group - 1 + (clips - 1 if reduce else 0))
 
     def send(src, dst, ssem, rsem, u):
         return pltpu.make_async_remote_copy(
@@ -249,17 +346,34 @@
     n = frames * rows * wc
     mid = jnp.concatenate([mid32[0], mid32[1]], -1)
     diff = (mid - teacher[...].astype(F32).reshape(n, chan)).astype(BF16)
-    for k in range(3):
-        gt_out[pl.ds(k * chan, chan), :] = (
-            dot_t(spat[pl.ds(k, frames)].reshape(n, chan), diff) * scale_mid
-        )
+    grad = jnp.concatenate(
+        [dot_t(spat[pl.ds(k, frames)].reshape(n, chan), diff) * scale_mid for k in range(3)], 0
+    )
+    if reduce:
+        mid_sum = Sum(sums[:12], gt_out, grad, d, me, members, others, spaces)
+        mid_sum.first()
+    else:
+        gt_out[...] = grad
     own[2].wait()
     for f in peers:
         top_copy(f, f).wait_recv()
     diff_top = (
         student.astype(F32) - teacher_top[...].astype(F32).reshape(frames * points, width)
     ).astype(BF16)
-    go_out[...] = dot_t(attended, diff_top) * scale_top
+    grad = dot_t(attended, diff_top) * scale_top
+    if reduce:
+        top_sum = Sum(sums[12:], go_out, grad, d, me, members, others, spaces)
+        top_sum.first()
+        mid_sum.second()
+        top_sum.second()
+        mid_sum.third()
+        top_sum.third()
+        mid_sum.fourth()
+        top_sum.fourth()
+        mid_sum.finish()
+        top_sum.finish()
+    else:
+        go_out[...] = grad
 
     keep.wait()
     for u in peers:
@@ -294,12 +408,16 @@
     scale_mid = 1.0 / math.sqrt(rows * cols * devices_all)
     scale_top = 1.0 / math.sqrt(half_rows * half_cols * devices_all)
     dma = pltpu.SemaphoreType.DMA
+    group, clips = frames * spaces, lax.axis_size("dp")
+    grads = (w_temporal.shape, w_out.shape)
+    reduce = clips == 4 and all(r % (32 * group) == 0 and c % 256 == 0 for r, c in grads)
+    pieces = [(r // group, c) if reduce else (r, c) for r, c in grads]
     student, gt, go = pl.pallas_call(
-        functools.partial(kernel, frames, spaces, scale_mid, scale_top),
+        functools.partial(kernel, frames, spaces, clips, reduce, scale_mid, scale_top),
         out_shape=(
             jax.ShapeDtypeStruct((half_rows, frames, hc, width), BF16),
-            jax.ShapeDtypeStruct(w_temporal.shape, F32),
-            jax.ShapeDtypeStruct(w_out.shape, F32),
+            jax.ShapeDtypeStruct(pieces[0], F32),
+            jax.ShapeDtypeStruct(pieces[1], F32),
         ),
         in_specs=[pl.BlockSpec(memory_space=pl.ANY)] * 10,
         out_specs=(
@@ -330,9 +448,10 @@
             dma((4,)),
         ]
         + [dma((frames,))] * 10
-        + [dma((4,)), dma((4,))],
+        + [dma((4,)), dma((4,))]
+        + (sum_scratch(grads[0], group, clips) + sum_scratch(grads[1], group, clips) if reduce else []),
         compiler_params=pltpu.CompilerParams(
-            collective_id=0, has_side_effects=True, vmem_limit_bytes=40 * 1024 * 1024
+            collective_id=0, has_side_effects=True, vmem_limit_bytes=58 * 1024 * 1024
         ),
     )(
         feats.reshape(rows, frames, wc, chan),
@@ -346,10 +465,11 @@
         w_out,
         teacher_top.reshape(half_rows, frames, hc, width),
     )
-    share_t = lax.psum_scatter(gt, ("tm", "space"), scatter_dimension=0, tiled=True)
-    share_o = lax.psum_scatter(go, ("tm", "space"), scatter_dimension=0, tiled=True)
-    grad_t, grad_o = lax.psum((share_t, share_o), "dp")
-    return (student.reshape(1, 1, half_rows, half_cols, width), grad_t, grad_o)
+    if not reduce:
+        gt = lax.psum_scatter(gt, ("tm", "space"), scatter_dimension=0, tiled=True)
+        go = lax.psum_scatter(go, ("tm", "space"), scatter_dimension=0, tiled=True)
+        gt, go = lax.psum((gt, go), "dp")
+    return (student.reshape(1, 1, half_rows, half_cols, width), gt, go)
 
 
 def solution(mesh):

time: 235 us -> 62.4 us (0.27)
  waiting for transfers between devices: 164 us -> 0 us
  Pallas kernels: 42.3 us -> 56.8 us
  between operations: 13.8 us -> 0.64 us
  local copies, waits for them, and re-layouts: 14.5 us -> 4.78 us
    reduce_scatter x2 -> x0, waiting for transfers between devices: 130 us -> none  [the longest x1 66.2 us: local(): lax.psum_scatter(go, ('tm', 'space'), scatter_dimension=0, tiled=True)]
    psum x1 -> x0, waiting for transfers between devices: 33.4 us -> none  [local(): grad_t, grad_o = lax.psum((share_t, share_o), 'dp')]
    pallas_call x1, Pallas kernels: 42.3 us -> 56.8 us  [local(): pl.pallas_call(functools.partial(kernel, frames, spaces, clips, reduce, s...]
    unnamed x23 -> x3, local copies, waits for them, and re-layouts: 14.5 us -> 4.78 us
  transfers between devices with their start and end apart: 3 -> 0, of which waited for: 3 -> 0; matrix products, arithmetic and copies ran while one was open for 0% -> 0% of each run, Pallas kernels for 0% -> 0%
where the time goes in v2:
time: 62.4 us; the launch traced here: 62.2 us
  Pallas kernels  56.8 us (91%)
  local copies, waits for them, and re-layouts  4.78 us (8%)
  between operations  0.64 us (1%)
    pallas_call x1, Pallas kernels, local(): pl.pallas_call(functools.partial(kernel, frames, spaces, clips, reduce, s...  56.8 us
    unnamed x3, local copies, waits for them, and re-layouts  4.78 us

profile of v2, /device:TPU:0, one launch (start us, length us, event | category | flops | bytes accessed | tf_op | source)
XLA Modules:
  0.0 62.2 jit_solution(3186037279299893155)
XLA Ops:
  0.6 56.8 %shard_map.121 = (bf16[4,4,16,512]{3,2,1,0:T(8,128)(2,1)}, f32[96,256]{1,0:T(8,128)}, f32[64,512]{1,0:T(8,128)}) custom-call(bf16[8,4,32,256]{3,2,1,0:T(8,128)(2,1)} %bitcast.6, bf16[3,768,256]{2,1,0:T(8,128)(2,1)} %bitcast.5, bf16[768,256]{1,0:T(8,128)(2,1)} %w_tm.1, bf16[8,4,32,256]{3,2,1,0:T(8,128)(2,1)} %bitcast.7, bf16[2,2,256,512]{3,2,1,0:T(8,128)(2,1)} %w_dn.1, ...), custom_call_target="tpu_custom_call" | custom-call | tf_op jit(solution)/shard_map/pallas_call | solution.py:415
  57.4 1.7 %copy.16 = bf16[1,1,4,64,512]{4,3,2,1,0:T(8,128)(2,1)} copy(bf16[1,1,4,64,512]{4,3,2,1,0:T(8,128)(2,1)} %bitcast.9) | data formatting | bytes 524288
  59.1 1.5 %copy.17 = f32[96,256]{1,0:T(8,128)} copy(f32[96,256]{1,0:T(8,128)} %get-tuple-element.13) | data formatting | bytes 196608
  60.7 1.6 %copy.18 = f32[64,512]{1,0:T(8,128)} copy(f32[64,512]{1,0:T(8,128)} %get-tuple-element.14) | data formatting | bytes 262144

commit v3 on v2

--- a/solution.py
+++ b/solution.py
@@ -78,7 +78,7 @@
     def fourth(self):
         for g in self.members:
             self.three(g, g).wait_recv()
-        self.done[self.d] = jnp.sum(self.in3[...].astype(F32), 0)
+        self.done[self.d] = jnp.sum(self.in3[...].astype(F32), 0).astype(BF16)
         for c in self.others:
             self.four(c, self.d).start()
 
@@ -87,7 +87,7 @@
             self.four(c, c).wait_recv()
         count, rows, cols = self.done.shape
         for c in range(count):
-            self.out[pl.ds((c % 2) * rows, rows), pl.ds((c // 2) * cols, cols)] = self.done[c]
+            self.out[pl.ds((c % 2) * rows, rows), pl.ds((c // 2) * cols, cols)] = self.done[c].astype(F32)
         self.one().wait_send()
         self.two().wait_send()
         for g in self.members:
@@ -106,7 +106,7 @@
         pltpu.VMEM((group, rows, cols // 2), BF16),
         pltpu.VMEM((group, rows, cols // 2), BF16),
         pltpu.VMEM((group, rows, cols // 2), BF16),
-        pltpu.VMEM((clips, rows, cols // 2), F32),
+        pltpu.VMEM((clips, rows, cols // 2), BF16),
         dma((4,)),
         dma((group,)),
         dma((group,)),
@@ -219,8 +219,6 @@
         feats_copy(f, f).wait_recv()
     for u in peers:
         teach_copy(u, t).start()
-    for u in peers:
-        top_copy(u, t).start()
 
     def halo(src, dst, i, j, to):
         return pltpu.make_async_remote_copy(
@@ -272,8 +270,7 @@
     for r in range(rows):
         shift(r + 1, side[:, r:r + 1, :], side[:, rows + r:rows + r + 1, :])
     loads[1].wait()
-    for first in range(1, rows - 1, 2):
-        conv(first, 2)
+    conv(1, rows - 2)
 
     @pl.when(s < spaces - 1)
     def _():
@@ -294,15 +291,17 @@
 
     loads[2].wait()
     half = chan // 2
+    n = frames * rows * wc
+    total = None
+    for k in range(3):
+        term = dot(spat[pl.ds(k, frames)].reshape(n, chan), v_tm[pl.ds(k * chan, chan), :])
+        total = term if total is None else total + term
     for f in range(frames):
-        total = None
-        for k in range(3):
-            term = dot(spat[f + k].reshape(rows * wc, chan), v_tm[pl.ds(k * chan, chan), :])
-            total = term if total is None else total + term
         base = cells[pl.ds(1, rows), f].astype(F32).reshape(rows * wc, chan)
-        mid = (base + total).astype(BF16).astype(F32)
+        span = slice(f * rows * wc, (f + 1) * rows * wc)
+        mid = (base + total[span]).astype(BF16).astype(F32)
         for h in range(2):
-            mid32[h, pl.ds(f * rows * wc, rows * wc), :] = mid[:, h * half:(h + 1) * half]
+            mid32[h, span, :] = mid[:, h * half:(h + 1) * half]
 
     loads[3].wait()
     coarse = None
@@ -335,15 +334,14 @@
     attended = jnp.concatenate(results, 0).astype(BF16)
     student = (coarse.astype(F32) + dot(attended, v_o[...])).astype(BF16)
     stu[...] = student.reshape(frames, half_rows, hc, width)
-    for u in peers:
-        student_copy(u, t).start()
     keep = pltpu.make_async_copy(stu.at[t], student_out.at[:, t], own_sem.at[3])
     keep.start()
 
     own[1].wait()
     for f in peers:
         teach_copy(f, f).wait_recv()
-    n = frames * rows * wc
+    for u in peers:
+        top_copy(u, t).start()
     mid = jnp.concatenate([mid32[0], mid32[1]], -1)
     diff = (mid - teacher[...].astype(F32).reshape(n, chan)).astype(BF16)
     grad = jnp.concatenate(
@@ -357,6 +355,8 @@
     own[2].wait()
     for f in peers:
         top_copy(f, f).wait_recv()
+    for u in peers:
+        student_copy(u, t).start()
     diff_top = (
         student.astype(F32) - teacher_top[...].astype(F32).reshape(frames * points, width)
     ).astype(BF16)
@@ -394,6 +394,18 @@
     def _():
         for copy in down(s + 1):
             copy.wait_send()
+
+
+def hand_over(*refs):
+    count = len(refs) // 2
+    sems = refs[-1]
+    copies = [
+        pltpu.make_async_copy(refs[i], refs[count + i], sems.at[i]) for i in range(count)
+    ]
+    for copy in copies:
+        copy.start()
+    for copy in copies:
+        copy.wait()
 
 
 def local(
@@ -465,7 +477,16 @@
         w_out,
         teacher_top.reshape(half_rows, frames, hc, width),
     )
-    if not reduce:
+    if reduce:
+        student, gt, go = pl.pallas_call(
+            hand_over,
+            out_shape=tuple(jax.ShapeDtypeStruct(x.shape, x.dtype) for x in (student, gt, go)),
+            in_specs=[pl.BlockSpec(memory_space=pl.ANY)] * 3,
+            out_specs=(pl.BlockSpec(memory_space=pl.ANY),) * 3,
+            scratch_shapes=[dma((3,))],
+            compiler_params=pltpu.CompilerParams(vmem_limit_bytes=58 * 1024 * 1024),
+        )(student, gt, go)
+    else:
         gt = lax.psum_scatter(gt, ("tm", "space"), scatter_dimension=0, tiled=True)
         go = lax.psum_scatter(go, ("tm", "space"), scatter_dimension=0, tiled=True)
         gt, go = lax.psum((gt, go), "dp")

time: 62.4 us -> 73.4 us (1.18)
  Pallas kernels: 56.8 us -> 72.6 us
  local copies, waits for them, and re-layouts: 4.78 us -> 0 us
    pallas_call x0 -> x1, Pallas kernels: none -> 16 us  [local(): pl.pallas_call(hand_over, out_shape=tuple((jax.ShapeDtypeStruct(x.shape,...]
    unnamed x3 -> x0, local copies, waits for them, and re-layouts: 4.78 us -> none
where the time goes in v3:
time: 73.4 us; the launch traced here: 73.3 us
  Pallas kernels  72.6 us (99%)
    pallas_call x1, Pallas kernels, local(): pl.pallas_call(functools.partial(kernel, frames, spaces, clips, reduce, s...  56.6 us
    pallas_call x1, Pallas kernels, local(): pl.pallas_call(hand_over, out_shape=tuple((jax.ShapeDtypeStruct(x.shape,...  16 us

profile of v3, /device:TPU:0, one launch (start us, length us, event | category | flops | bytes accessed | tf_op | source)
XLA Modules:
  0.0 73.3 jit_solution(8841881016272533689)
XLA Ops:
  0.6 56.6 %shard_map.121 = (bf16[4,4,16,512]{3,2,1,0:T(8,128)(2,1)}, f32[96,256]{1,0:T(8,128)}, f32[64,512]{1,0:T(8,128)}) custom-call(bf16[8,4,32,256]{3,2,1,0:T(8,128)(2,1)} %bitcast.6, bf16[3,768,256]{2,1,0:T(8,128)(2,1)} %bitcast.5, bf16[768,256]{1,0:T(8,128)(2,1)} %w_tm.1, bf16[8,4,32,256]{3,2,1,0:T(8,128)(2,1)} %bitcast.7, bf16[2,2,256,512]{3,2,1,0:T(8,128)(2,1)} %w_dn.1, ...), custom_call_target="tpu_custom_call" | custom-call | tf_op jit(solution)/shard_map/pallas_call | solution.py:427
  57.3 16.0 %shard_map.122 = (bf16[4,4,16,512]{3,2,1,0:T(8,128)(2,1)}, f32[96,256]{1,0:T(8,128)}, f32[64,512]{1,0:T(8,128)}) custom-call(bf16[4,4,16,512]{3,2,1,0:T(8,128)(2,1)} %get-tuple-element.9.refs_0_, f32[96,256]{1,0:T(8,128)} %get-tuple-element.10.refs_1_, f32[64,512]{1,0:T(8,128)} %get-tuple-element.11.refs_2_), custom_call_target="tpu_custom_call" | custom-call | tf_op jit(solution)/shard_map/pallas_call | solution.py:481

commit v4 on v3

--- a/solution.py
+++ b/solution.py
@@ -15,10 +15,6 @@
 
 def dot(a, b):
     return jnp.dot(a, b, preferred_element_type=F32)
-
-
-def dot_t(a, b):
-    return lax.dot_general(a, b, (((0,), (0,)), ((), ())), preferred_element_type=F32)
 
 
 class Sum:
@@ -120,7 +116,7 @@
     feats, w_sp, w_tm, teach, w_dn, w_q, w_k, w_v, w_o, teach_top,
     student_out, gt_out, go_out,
     home, v_sp, v_tm, v_dn, v_q, v_k, v_v, v_o,
-    cells, edge_send, edges, edge_near, shifted, spat, teacher, teacher_top, mid32, stu,
+    cells, edge_send, edges, edge_near, shifted, spat, turned, teacher, teacher_top, mid32, stu,
     in_sem, own_sem, fs, fr, es, er, ts, tr, ps, pr_, ss, sr, hs, hr,
     *sums,
 ):
@@ -188,8 +184,10 @@
     def edge_copy(u, f):
         return send(edge_send.at[u], edges.at[f], es.at[u], er.at[f], u)
 
-    def teach_copy(u, f):
-        return send(teach.at[:, u], teacher.at[f], ts.at[u], tr.at[f], u)
+    def teach_copy(u, f, h):
+        part = pl.ds(h * (rows // 2), rows // 2)
+        return send(teach.at[part, u], teacher.at[f, part],
+                    ts.at[h * frames + u], tr.at[h * frames + f], u)
 
     def top_copy(u, f):
         return send(teach_top.at[:, u], teacher_top.at[f], ps.at[u], pr_.at[f], u)
@@ -218,7 +216,10 @@
         edge_copy(f, f).wait_recv()
         feats_copy(f, f).wait_recv()
     for u in peers:
-        teach_copy(u, t).start()
+        top_copy(u, t).start()
+    for h in range(2):
+        for u in peers:
+            teach_copy(u, t, h).start()
 
     def halo(src, dst, i, j, to):
         return pltpu.make_async_remote_copy(
@@ -337,43 +338,56 @@
     keep = pltpu.make_async_copy(stu.at[t], student_out.at[:, t], own_sem.at[3])
     keep.start()
 
+    for u in peers:
+        student_copy(u, t).start()
+
+    turned_top = attended.T
+    own[2].wait()
+    for f in peers:
+        top_copy(f, f).wait_recv()
+    diff_top = (
+        student.astype(F32) - teacher_top[...].astype(F32).reshape(frames * points, width)
+    ).astype(BF16)
+    grad_top = dot(turned_top, diff_top) * scale_top
+    if reduce:
+        top_sum = Sum(sums[12:], go_out, grad_top, d, me, members, others, spaces)
+        top_sum.first()
+    else:
+        go_out[...] = grad_top
+
+    low = rows // 2
+    for h in range(2):
+        for k in range(3):
+            part = spat[pl.ds(k, frames), pl.ds(h * low, low)]
+            turned[h, k] = part.reshape(n // 2, chan).T
+    if reduce:
+        top_sum.second()
     own[1].wait()
-    for f in peers:
-        teach_copy(f, f).wait_recv()
-    for u in peers:
-        top_copy(u, t).start()
-    mid = jnp.concatenate([mid32[0], mid32[1]], -1)
-    diff = (mid - teacher[...].astype(F32).reshape(n, chan)).astype(BF16)
-    grad = jnp.concatenate(
-        [dot_t(spat[pl.ds(k, frames)].reshape(n, chan), diff) * scale_mid for k in range(3)], 0
-    )
+    grad = [None] * 3
+    for h in range(2):
+        for f in peers:
+            teach_copy(f, f, h).wait_recv()
+        mid = jnp.concatenate(
+            [mid32[i].reshape(frames, 2, low * wc, half)[:, h] for i in range(2)], -1
+        ).reshape(n // 2, chan)
+        diff = mid - teacher[:, pl.ds(h * low, low)].astype(F32).reshape(n // 2, chan)
+        for k in range(3):
+            term = dot(turned[h, k], diff.astype(BF16))
+            grad[k] = term if h == 0 else grad[k] + term
+        if reduce and h == 0:
+            top_sum.third()
+    grad = jnp.concatenate(grad, 0) * scale_mid
     if reduce:
         mid_sum = Sum(sums[:12], gt_out, grad, d, me, members, others, spaces)
         mid_sum.first()
+        top_sum.fourth()
+        mid_sum.second()
+        mid_sum.third()
+        top_sum.finish()
+        mid_sum.fourth()
+        mid_sum.finish()
     else:
         gt_out[...] = grad
-    own[2].wait()
-    for f in peers:
-        top_copy(f, f).wait_recv()
-    for u in peers:
-        student_copy(u, t).start()
-    diff_top = (
-        student.astype(F32) - teacher_top[...].astype(F32).reshape(frames * points, width)
-    ).astype(BF16)
-    grad = dot_t(attended, diff_top) * scale_top
-    if reduce:
-        top_sum = Sum(sums[12:], go_out, grad, d, me, members, others, spaces)
-        top_sum.first()
-        mid_sum.second()
-        top_sum.second()
-        mid_sum.third()
-        top_sum.third()
-        mid_sum.fourth()
-        top_sum.fourth()
-        mid_sum.finish()
-        top_sum.finish()
-    else:
-        go_out[...] = grad
 
     keep.wait()
     for u in peers:
@@ -381,7 +395,8 @@
     for u in peers:
         edge_copy(u, t).wait_send()
         feats_copy(u, t).wait_send()
-        teach_copy(u, t).wait_send()
+        for h in range(2):
+            teach_copy(u, t, h).wait_send()
         top_copy(u, t).wait_send()
         student_copy(u, t).wait_send()
 
@@ -397,14 +412,16 @@
 
 
 def hand_over(*refs):
-    count = len(refs) // 2
-    sems = refs[-1]
-    copies = [
-        pltpu.make_async_copy(refs[i], refs[count + i], sems.at[i]) for i in range(count)
-    ]
-    for copy in copies:
+    count = (len(refs) - 1) // 3
+    ins, outs, held, sems = refs[:count], refs[count:2 * count], refs[2 * count:-1], refs[-1]
+    reads = [pltpu.make_async_copy(ins[i], held[i], sems.at[0, i]) for i in range(count)]
+    writes = [pltpu.make_async_copy(held[i], outs[i], sems.at[1, i]) for i in range(count)]
+    for copy in reads:
         copy.start()
-    for copy in copies:
+    for i in range(count):
+        reads[i].wait()
+        writes[i].start()
+    for copy in writes:
         copy.wait()
 
 
@@ -452,6 +469,7 @@
             pltpu.VMEM((2, frames, 2 * rows, chan), BF16),
             pltpu.VMEM((rows + 2, frames * wc, 3 * chan), BF16),
             pltpu.VMEM((frames + 2, rows, wc, chan), BF16),
+            pltpu.VMEM((2, 3, chan, frames * rows * wc // 2), BF16),
             pltpu.VMEM((frames, rows, wc, chan), BF16),
             pltpu.VMEM((frames, half_rows, hc, width), BF16),
             pltpu.VMEM((2, frames * rows * wc, chan // 2), F32),
@@ -459,7 +477,9 @@
             dma((8,)),
             dma((4,)),
         ]
-        + [dma((frames,))] * 10
+        + [dma((frames,))] * 4
+        + [dma((2 * frames,))] * 2
+        + [dma((frames,))] * 4
         + [dma((4,)), dma((4,))]
         + (sum_scratch(grads[0], group, clips) + sum_scratch(grads[1], group, clips) if reduce else []),
         compiler_params=pltpu.CompilerParams(
@@ -483,7 +503,8 @@
             out_shape=tuple(jax.ShapeDtypeStruct(x.shape, x.dtype) for x in (student, gt, go)),
             in_specs=[pl.BlockSpec(memory_space=pl.ANY)] * 3,
             out_specs=(pl.BlockSpec(memory_space=pl.ANY),) * 3,
-            scratch_shapes=[dma((3,))],
+            scratch_shapes=[pltpu.VMEM(x.shape, x.dtype) for x in (student, gt, go)]
+            + [dma((2, 3))],
             compiler_params=pltpu.CompilerParams(vmem_limit_bytes=58 * 1024 * 1024),
         )(student, gt, go)
     else:

time: 73.4 us -> 61.3 us (0.84)
  Pallas kernels: 72.6 us -> 60.5 us
    pallas_call x1, Pallas kernels: 16 us -> 1.78 us  [local(): pl.pallas_call(hand_over, out_shape=tuple((jax.ShapeDtypeStruct(x.shape,...]
    pallas_call x1, Pallas kernels: 56.6 us -> 58.7 us  [local(): pl.pallas_call(functools.partial(kernel, frames, spaces, clips, reduce, s...]
where the time goes in v4:
time: 61.3 us; the launch traced here: 61.1 us
  Pallas kernels  60.5 us (99%)
  between operations  0.64 us (1%)
    pallas_call x1, Pallas kernels, local(): pl.pallas_call(functools.partial(kernel, frames, spaces, clips, reduce, s...  58.7 us
    pallas_call x1, Pallas kernels, local(): pl.pallas_call(hand_over, out_shape=tuple((jax.ShapeDtypeStruct(x.shape,...  1.78 us

profile of v4, /device:TPU:0, one launch (start us, length us, event | category | flops | bytes accessed | tf_op | source)
XLA Modules:
  0.0 61.1 jit_solution(13759910910120225641)
XLA Ops:
  0.6 58.7 %shard_map.121 = (bf16[4,4,16,512]{3,2,1,0:T(8,128)(2,1)}, f32[96,256]{1,0:T(8,128)}, f32[64,512]{1,0:T(8,128)}) custom-call(bf16[8,4,32,256]{3,2,1,0:T(8,128)(2,1)} %bitcast.6, bf16[3,768,256]{2,1,0:T(8,128)(2,1)} %bitcast.5, bf16[768,256]{1,0:T(8,128)(2,1)} %w_tm.1, bf16[8,4,32,256]{3,2,1,0:T(8,128)(2,1)} %bitcast.7, bf16[2,2,256,512]{3,2,1,0:T(8,128)(2,1)} %w_dn.1, ...), custom_call_target="tpu_custom_call" | custom-call | tf_op jit(solution)/shard_map/pallas_call | solution.py:444
  59.3 1.8 %shard_map.122 = (bf16[4,4,16,512]{3,2,1,0:T(8,128)(2,1)}, f32[96,256]{1,0:T(8,128)}, f32[64,512]{1,0:T(8,128)}) custom-call(bf16[4,4,16,512]{3,2,1,0:T(8,128)(2,1)} %get-tuple-element.9.refs_0_, f32[96,256]{1,0:T(8,128)} %get-tuple-element.10.refs_1_, f32[64,512]{1,0:T(8,128)} %get-tuple-element.11.refs_2_), custom_call_target="tpu_custom_call" | custom-call | tf_op jit(solution)/shard_map/pallas_call | solution.py:501

commit v5 on v4

--- a/solution.py
+++ b/solution.py
@@ -338,8 +338,6 @@
     keep = pltpu.make_async_copy(stu.at[t], student_out.at[:, t], own_sem.at[3])
     keep.start()
 
-    for u in peers:
-        student_copy(u, t).start()
 
     turned_top = attended.T
     own[2].wait()
@@ -367,6 +365,9 @@
     for h in range(2):
         for f in peers:
             teach_copy(f, f, h).wait_recv()
+        if h == 1:
+            for u in peers:
+                student_copy(u, t).start()
         mid = jnp.concatenate(
             [mid32[i].reshape(frames, 2, low * wc, half)[:, h] for i in range(2)], -1
         ).reshape(n // 2, chan)

time: 61.3 us -> 58.7 us (0.958)
  Pallas kernels: 60.5 us -> 57.9 us
    pallas_call x1, Pallas kernels: 58.7 us -> 56.2 us  [local(): pl.pallas_call(functools.partial(kernel, frames, spaces, clips, reduce, s...]
where the time goes in v5:
time: 58.7 us; the launch traced here: 58.6 us
  Pallas kernels  57.9 us (99%)
  between operations  0.64 us (1%)
    pallas_call x1, Pallas kernels, local(): pl.pallas_call(functools.partial(kernel, frames, spaces, clips, reduce, s...  56.2 us
    pallas_call x1, Pallas kernels, local(): pl.pallas_call(hand_over, out_shape=tuple((jax.ShapeDtypeStruct(x.shape,...  1.78 us

profile of v5, /device:TPU:0, one launch (start us, length us, event | category | flops | bytes accessed | tf_op | source)
XLA Modules:
  0.0 58.6 jit_solution(7629861811754922398)
XLA Ops:
  0.6 56.2 %shard_map.121 = (bf16[4,4,16,512]{3,2,1,0:T(8,128)(2,1)}, f32[96,256]{1,0:T(8,128)}, f32[64,512]{1,0:T(8,128)}) custom-call(bf16[8,4,32,256]{3,2,1,0:T(8,128)(2,1)} %bitcast.6, bf16[3,768,256]{2,1,0:T(8,128)(2,1)} %bitcast.5, bf16[768,256]{1,0:T(8,128)(2,1)} %w_tm.1, bf16[8,4,32,256]{3,2,1,0:T(8,128)(2,1)} %bitcast.7, bf16[2,2,256,512]{3,2,1,0:T(8,128)(2,1)} %w_dn.1, ...), custom_call_target="tpu_custom_call" | custom-call | tf_op jit(solution)/shard_map/pallas_call | solution.py:445
  56.8 1.8 %shard_map.122 = (bf16[4,4,16,512]{3,2,1,0:T(8,128)(2,1)}, f32[96,256]{1,0:T(8,128)}, f32[64,512]{1,0:T(8,128)}) custom-call(bf16[4,4,16,512]{3,2,1,0:T(8,128)(2,1)} %get-tuple-element.9.refs_0_, f32[96,256]{1,0:T(8,128)} %get-tuple-element.10.refs_1_, f32[64,512]{1,0:T(8,128)} %get-tuple-element.11.refs_2_), custom_call_target="tpu_custom_call" | custom-call | tf_op jit(solution)/shard_map/pallas_call | solution.py:502

commit v6 on v5

--- a/solution.py
+++ b/solution.py
@@ -115,7 +115,7 @@
     frames, spaces, clips, reduce, scale_mid, scale_top,
     feats, w_sp, w_tm, teach, w_dn, w_q, w_k, w_v, w_o, teach_top,
     student_out, gt_out, go_out,
-    home, v_sp, v_tm, v_dn, v_q, v_k, v_v, v_o,
+    home, home_teach, home_top, v_sp, v_tm, v_dn, v_q, v_k, v_v, v_o,
     cells, edge_send, edges, edge_near, shifted, spat, turned, teacher, teacher_top, mid32, stu,
     in_sem, own_sem, fs, fr, es, er, ts, tr, ps, pr_, ss, sr, hs, hr,
     *sums,
@@ -135,7 +135,8 @@
         pltpu.make_async_copy(src, dst, in_sem.at[i])
         for i, (src, dst) in enumerate(
             ((feats, home), (w_sp, v_sp), (w_tm, v_tm), (w_dn, v_dn),
-             (w_q, v_q), (w_k, v_k), (w_v, v_v), (w_o, v_o))
+             (w_q, v_q), (w_k, v_k), (w_v, v_v), (w_o, v_o),
+             (teach_top, home_top), (teach, home_teach))
         )
     ]
     for load in loads:
@@ -186,11 +187,11 @@
 
     def teach_copy(u, f, h):
         part = pl.ds(h * (rows // 2), rows // 2)
-        return send(teach.at[part, u], teacher.at[f, part],
+        return send(home_teach.at[part, u], teacher.at[f, part],
                     ts.at[h * frames + u], tr.at[h * frames + f], u)
 
     def top_copy(u, f):
-        return send(teach_top.at[:, u], teacher_top.at[f], ps.at[u], pr_.at[f], u)
+        return send(home_top.at[:, u], teacher_top.at[f], ps.at[u], pr_.at[f], u)
 
     def student_copy(u, f):
         return send(stu.at[u], student_out.at[:, f], ss.at[u], sr.at[f], u)
@@ -215,8 +216,10 @@
     for f in peers:
         edge_copy(f, f).wait_recv()
         feats_copy(f, f).wait_recv()
+    loads[8].wait()
     for u in peers:
         top_copy(u, t).start()
+    loads[9].wait()
     for h in range(2):
         for u in peers:
             teach_copy(u, t, h).start()
@@ -450,13 +453,11 @@
             jax.ShapeDtypeStruct(pieces[1], F32),
         ),
         in_specs=[pl.BlockSpec(memory_space=pl.ANY)] * 10,
-        out_specs=(
-            pl.BlockSpec(memory_space=pl.ANY),
-            pl.BlockSpec(memory_space=pltpu.VMEM),
-            pl.BlockSpec(memory_space=pltpu.VMEM),
-        ),
+        out_specs=(pl.BlockSpec(memory_space=pltpu.VMEM),) * 3,
         scratch_shapes=[
             pltpu.VMEM((rows, frames, wc, chan), BF16),
+            pltpu.VMEM((rows, frames, wc, chan), BF16),
+            pltpu.VMEM((half_rows, frames, hc, width), BF16),
             pltpu.VMEM((3, 3 * chan, chan), BF16),
             pltpu.VMEM(w_temporal.shape, BF16),
             pltpu.VMEM(w_down.shape, BF16),
@@ -475,7 +476,7 @@
             pltpu.VMEM((frames, half_rows, hc, width), BF16),
             pltpu.VMEM((2, frames * rows * wc, chan // 2), F32),
             pltpu.VMEM((frames, half_rows, hc, width), BF16),
-            dma((8,)),
+            dma((10,)),
             dma((4,)),
         ]
         + [dma((frames,))] * 4

time: 58.7 us -> 58.4 us (level)
  no operation moved by 1% of the time
where the time goes in v6:
time: 58.4 us; the launch traced here: 58.3 us
  Pallas kernels  57.6 us (99%)
  between operations  0.64 us (1%)
    pallas_call x1, Pallas kernels, local(): pl.pallas_call(functools.partial(kernel, frames, spaces, clips, reduce, s...  55.8 us
    pallas_call x1, Pallas kernels, local(): pl.pallas_call(hand_over, out_shape=tuple((jax.ShapeDtypeStruct(x.shape,...  1.78 us

profile of v6, /device:TPU:0, one launch (start us, length us, event | category | flops | bytes accessed | tf_op | source)
XLA Modules:
  0.0 58.3 jit_solution(1468869097832597454)
XLA Ops:
  0.6 55.8 %shard_map.121 = (bf16[4,4,16,512]{3,2,1,0:T(8,128)(2,1)}, f32[96,256]{1,0:T(8,128)}, f32[64,512]{1,0:T(8,128)}) custom-call(bf16[8,4,32,256]{3,2,1,0:T(8,128)(2,1)} %bitcast.6, bf16[3,768,256]{2,1,0:T(8,128)(2,1)} %bitcast.5, bf16[768,256]{1,0:T(8,128)(2,1)} %w_tm.1, bf16[8,4,32,256]{3,2,1,0:T(8,128)(2,1)} %bitcast.7, bf16[2,2,256,512]{3,2,1,0:T(8,128)(2,1)} %w_dn.1, ...), custom_call_target="tpu_custom_call" | custom-call | tf_op jit(solution)/shard_map/pallas_call | solution.py:448
  56.5 1.8 %shard_map.122 = (bf16[4,4,16,512]{3,2,1,0:T(8,128)(2,1)}, f32[96,256]{1,0:T(8,128)}, f32[64,512]{1,0:T(8,128)}) custom-call(bf16[4,4,16,512]{3,2,1,0:T(8,128)(2,1)} %get-tuple-element.9.refs_0_, f32[96,256]{1,0:T(8,128)} %get-tuple-element.10.refs_1_, f32[64,512]{1,0:T(8,128)} %get-tuple-element.11.refs_2_), custom_call_target="tpu_custom_call" | custom-call | tf_op jit(solution)/shard_map/pallas_call | solution.py:503

commit v7 on v6

--- a/solution.py
+++ b/solution.py
@@ -115,7 +115,7 @@
     frames, spaces, clips, reduce, scale_mid, scale_top,
     feats, w_sp, w_tm, teach, w_dn, w_q, w_k, w_v, w_o, teach_top,
     student_out, gt_out, go_out,
-    home, home_teach, home_top, v_sp, v_tm, v_dn, v_q, v_k, v_v, v_o,
+    home, home_teach, v_sp, v_tm, v_dn, v_q, v_k, v_v, v_o,
     cells, edge_send, edges, edge_near, shifted, spat, turned, teacher, teacher_top, mid32, stu,
     in_sem, own_sem, fs, fr, es, er, ts, tr, ps, pr_, ss, sr, hs, hr,
     *sums,
@@ -136,19 +136,14 @@
         for i, (src, dst) in enumerate(
             ((feats, home), (w_sp, v_sp), (w_tm, v_tm), (w_dn, v_dn),
              (w_q, v_q), (w_k, v_k), (w_v, v_v), (w_o, v_o),
-             (teach_top, home_top), (teach, home_teach))
+             (teach, home_teach))
         )
     ]
-    for load in loads:
-        load.start()
     own = [
         pltpu.make_async_copy(feats.at[:, t], cells.at[pl.ds(1, rows), t], own_sem.at[0]),
         pltpu.make_async_copy(teach.at[:, t], teacher.at[t], own_sem.at[1]),
         pltpu.make_async_copy(teach_top.at[:, t], teacher_top.at[t], own_sem.at[2]),
     ]
-    for copy in own:
-        copy.start()
-
     barrier = pltpu.get_barrier_semaphore()
     for g in members:
         pl.semaphore_signal(
@@ -158,6 +153,39 @@
     if reduce:
         for c in others:
             pl.semaphore_signal(barrier, inc=1, device_id={"dp": c}, device_id_type=MESH)
+
+    loads[0].start()
+
+    def send(src, dst, ssem, rsem, u):
+        return pltpu.make_async_remote_copy(
+            src_ref=src, dst_ref=dst, send_sem=ssem, recv_sem=rsem,
+            device_id={"tm": u}, device_id_type=MESH,
+        )
+
+    def feats_copy(u, f):
+        return send(feats.at[:, u], cells.at[pl.ds(1, rows), f], fs.at[u], fr.at[f], u)
+
+    def edge_copy(u, f):
+        return send(edge_send.at[u], edges.at[f], es.at[u], er.at[f], u)
+
+    def teach_copy(u, f, h):
+        part = pl.ds(h * (rows // 2), rows // 2)
+        return send(home_teach.at[part, u], teacher.at[f, part],
+                    ts.at[h * frames + u], tr.at[h * frames + f], u)
+
+    def top_copy(u, f):
+        return send(teach_top.at[:, u], teacher_top.at[f], ps.at[u], pr_.at[f], u)
+
+    def student_copy(u, f):
+        return send(stu.at[u], student_out.at[:, f], ss.at[u], sr.at[f], u)
+
+    pl.semaphore_wait(barrier, group - 1 + (clips - 1 if reduce else 0))
+    for u in peers:
+        feats_copy(u, t).start()
+    for copy in own:
+        copy.start()
+    for load in loads[1:]:
+        load.start()
 
     loads[0].wait()
     for u in range(frames):
@@ -171,34 +199,10 @@
             right = jnp.zeros((rows, chan), F32)
         edge_send[u] = jnp.concatenate([left, right], 0).astype(BF16)
 
-    pl.semaphore_wait(barrier, group - 1 + (clips - 1 if reduce else 0))
-
-    def send(src, dst, ssem, rsem, u):
-        return pltpu.make_async_remote_copy(
-            src_ref=src, dst_ref=dst, send_sem=ssem, recv_sem=rsem,
-            device_id={"tm": u}, device_id_type=MESH,
-        )
-
-    def feats_copy(u, f):
-        return send(home.at[:, u], cells.at[pl.ds(1, rows), f], fs.at[u], fr.at[f], u)
-
-    def edge_copy(u, f):
-        return send(edge_send.at[u], edges.at[f], es.at[u], er.at[f], u)
-
-    def teach_copy(u, f, h):
-        part = pl.ds(h * (rows // 2), rows // 2)
-        return send(home_teach.at[part, u], teacher.at[f, part],
-                    ts.at[h * frames + u], tr.at[h * frames + f], u)
-
-    def top_copy(u, f):
-        return send(home_top.at[:, u], teacher_top.at[f], ps.at[u], pr_.at[f], u)
-
-    def student_copy(u, f):
-        return send(stu.at[u], student_out.at[:, f], ss.at[u], sr.at[f], u)
-
     for u in peers:
         edge_copy(u, t).start()
-        feats_copy(u, t).start()
+    for u in peers:
+        top_copy(u, t).start()
     edges[t] = edge_send[t]
     spat[pl.ds(0, 2)] = jnp.zeros((2,) + spat.shape[1:], BF16)
 
@@ -217,9 +221,6 @@
         edge_copy(f, f).wait_recv()
         feats_copy(f, f).wait_recv()
     loads[8].wait()
-    for u in peers:
-        top_copy(u, t).start()
-    loads[9].wait()
     for h in range(2):
         for u in peers:
             teach_copy(u, t, h).start()
@@ -457,7 +458,6 @@
         scratch_shapes=[
             pltpu.VMEM((rows, frames, wc, chan), BF16),
             pltpu.VMEM((rows, frames, wc, chan), BF16),
-            pltpu.VMEM((half_rows, frames, hc, width), BF16),
             pltpu.VMEM((3, 3 * chan, chan), BF16),
             pltpu.VMEM(w_temporal.shape, BF16),
             pltpu.VMEM(w_down.shape, BF16),
@@ -476,7 +476,7 @@
             pltpu.VMEM((frames, half_rows, hc, width), BF16),
             pltpu.VMEM((2, frames * rows * wc, chan // 2), F32),
             pltpu.VMEM((frames, half_rows, hc, width), BF16),
-            dma((10,)),
+            dma((9,)),
             dma((4,)),
         ]
         + [dma((frames,))] * 4

time: 58.4 us -> 58.8 us (level)
  no operation moved by 1% of the time
where the time goes in v7:
time: 58.8 us; the launch traced here: 58.6 us
  Pallas kernels  58 us (99%)
  between operations  0.64 us (1%)
    pallas_call x1, Pallas kernels, local(): pl.pallas_call(functools.partial(kernel, frames, spaces, clips, reduce, s...  56.2 us
    pallas_call x1, Pallas kernels, local(): pl.pallas_call(hand_over, out_shape=tuple((jax.ShapeDtypeStruct(x.shape,...  1.78 us

profile of v7, /device:TPU:0, one launch (start us, length us, event | category | flops | bytes accessed | tf_op | source)
XLA Modules:
  0.0 58.6 jit_solution(4064794743587678754)
XLA Ops:
  0.6 56.2 %shard_map.121 = (bf16[4,4,16,512]{3,2,1,0:T(8,128)(2,1)}, f32[96,256]{1,0:T(8,128)}, f32[64,512]{1,0:T(8,128)}) custom-call(bf16[8,4,32,256]{3,2,1,0:T(8,128)(2,1)} %bitcast.6, bf16[3,768,256]{2,1,0:T(8,128)(2,1)} %bitcast.5, bf16[768,256]{1,0:T(8,128)(2,1)} %w_tm.1, bf16[8,4,32,256]{3,2,1,0:T(8,128)(2,1)} %bitcast.7, bf16[2,2,256,512]{3,2,1,0:T(8,128)(2,1)} %w_dn.1, ...), custom_call_target="tpu_custom_call" | custom-call | tf_op jit(solution)/shard_map/pallas_call | solution.py:449
  56.8 1.8 %shard_map.122 = (bf16[4,4,16,512]{3,2,1,0:T(8,128)(2,1)}, f32[96,256]{1,0:T(8,128)}, f32[64,512]{1,0:T(8,128)}) custom-call(bf16[4,4,16,512]{3,2,1,0:T(8,128)(2,1)} %get-tuple-element.9.refs_0_, f32[96,256]{1,0:T(8,128)} %get-tuple-element.10.refs_1_, f32[64,512]{1,0:T(8,128)} %get-tuple-element.11.refs_2_), custom_call_target="tpu_custom_call" | custom-call | tf_op jit(solution)/shard_map/pallas_call | solution.py:503

commit v8 on v7

--- a/solution.py
+++ b/solution.py
@@ -115,7 +115,7 @@
     frames, spaces, clips, reduce, scale_mid, scale_top,
     feats, w_sp, w_tm, teach, w_dn, w_q, w_k, w_v, w_o, teach_top,
     student_out, gt_out, go_out,
-    home, home_teach, v_sp, v_tm, v_dn, v_q, v_k, v_v, v_o,
+    home, v_sp, v_tm, v_dn, v_q, v_k, v_v, v_o,
     cells, edge_send, edges, edge_near, shifted, spat, turned, teacher, teacher_top, mid32, stu,
     in_sem, own_sem, fs, fr, es, er, ts, tr, ps, pr_, ss, sr, hs, hr,
     *sums,
@@ -135,8 +135,7 @@
         pltpu.make_async_copy(src, dst, in_sem.at[i])
         for i, (src, dst) in enumerate(
             ((feats, home), (w_sp, v_sp), (w_tm, v_tm), (w_dn, v_dn),
-             (w_q, v_q), (w_k, v_k), (w_v, v_v), (w_o, v_o),
-             (teach, home_teach))
+             (w_q, v_q), (w_k, v_k), (w_v, v_v), (w_o, v_o))
         )
     ]
     own = [
@@ -168,10 +167,8 @@
     def edge_copy(u, f):
         return send(edge_send.at[u], edges.at[f], es.at[u], er.at[f], u)
 
-    def teach_copy(u, f, h):
-        part = pl.ds(h * (rows // 2), rows // 2)
-        return send(home_teach.at[part, u], teacher.at[f, part],
-                    ts.at[h * frames + u], tr.at[h * frames + f], u)
+    def teach_copy(u, f):
+        return send(teach.at[:, u], teacher.at[f], ts.at[u], tr.at[f], u)
 
     def top_copy(u, f):
         return send(teach_top.at[:, u], teacher_top.at[f], ps.at[u], pr_.at[f], u)
@@ -201,8 +198,6 @@
 
     for u in peers:
         edge_copy(u, t).start()
-    for u in peers:
-        top_copy(u, t).start()
     edges[t] = edge_send[t]
     spat[pl.ds(0, 2)] = jnp.zeros((2,) + spat.shape[1:], BF16)
 
@@ -220,10 +215,10 @@
     for f in peers:
         edge_copy(f, f).wait_recv()
         feats_copy(f, f).wait_recv()
-    loads[8].wait()
-    for h in range(2):
-        for u in peers:
-            teach_copy(u, t, h).start()
+    for u in peers:
+        top_copy(u, t).start()
+    for u in peers:
+        teach_copy(u, t).start()
 
     def halo(src, dst, i, j, to):
         return pltpu.make_async_remote_copy(
@@ -260,22 +255,28 @@
         shifted[row, :, pl.ds(chan, chan)] = cells[row].reshape(flat)
         shifted[row, :, pl.ds(2 * chan, chan)] = b.astype(BF16).reshape(flat)
 
-    def conv(first, count):
+    def conv(spans):
+        count = sum(c for _, c in spans)
         total = None
         for dy in range(3):
-            block = shifted[pl.ds(first + dy, count)].reshape(count * frames * wc, 3 * chan)
+            blocks = [
+                shifted[pl.ds(first + dy, c)].reshape(c * frames * wc, 3 * chan)
+                for first, c in spans
+            ]
+            block = blocks[0] if len(blocks) == 1 else jnp.concatenate(blocks, 0)
             term = dot(block, v_sp[dy])
             total = term if total is None else total + term
         out = (total / (1.0 + jnp.exp(-total))).astype(BF16)
         out = out.reshape(count, frames, wc, chan)
-        for i in range(count):
-            spat[pl.ds(2, frames), first + i] = out[i]
+        places = [first + i for first, c in spans for i in range(c)]
+        for i, row in enumerate(places):
+            spat[pl.ds(2, frames), row] = out[i]
 
     side = edges[...].astype(F32)
     for r in range(rows):
         shift(r + 1, side[:, r:r + 1, :], side[:, rows + r:rows + r + 1, :])
     loads[1].wait()
-    conv(1, rows - 2)
+    conv([(1, rows - 2)])
 
     @pl.when(s < spaces - 1)
     def _():
@@ -291,8 +292,7 @@
     shift(0, side[:, rows - 1:rows, :], side[:, 2 * rows - 1:2 * rows, :])
     side = edge_near[1].astype(F32)
     shift(rows + 1, side[:, 0:1, :], side[:, rows:rows + 1, :])
-    conv(0, 1)
-    conv(rows - 1, 1)
+    conv([(0, 1), (rows - 1, 1)])
 
     loads[2].wait()
     half = chan // 2
@@ -357,36 +357,27 @@
     else:
         go_out[...] = grad_top
 
-    low = rows // 2
-    for h in range(2):
-        for k in range(3):
-            part = spat[pl.ds(k, frames), pl.ds(h * low, low)]
-            turned[h, k] = part.reshape(n // 2, chan).T
+    frame = rows * wc
+    turned[:, pl.ds(0, 2 * frame)] = jnp.zeros((chan, 2 * frame), BF16)
+    for f in range(frames):
+        turned[:, pl.ds((f + 2) * frame, frame)] = spat[f + 2].reshape(frame, chan).T
     if reduce:
         top_sum.second()
     own[1].wait()
-    grad = [None] * 3
-    for h in range(2):
-        for f in peers:
-            teach_copy(f, f, h).wait_recv()
-        if h == 1:
-            for u in peers:
-                student_copy(u, t).start()
-        mid = jnp.concatenate(
-            [mid32[i].reshape(frames, 2, low * wc, half)[:, h] for i in range(2)], -1
-        ).reshape(n // 2, chan)
-        diff = mid - teacher[:, pl.ds(h * low, low)].astype(F32).reshape(n // 2, chan)
-        for k in range(3):
-            term = dot(turned[h, k], diff.astype(BF16))
-            grad[k] = term if h == 0 else grad[k] + term
-        if reduce and h == 0:
-            top_sum.third()
+    for f in peers:
+        teach_copy(f, f).wait_recv()
+    for u in peers:
+        student_copy(u, t).start()
+    mid = jnp.concatenate([mid32[0], mid32[1]], -1)
+    diff = (mid - teacher[...].astype(F32).reshape(n, chan)).astype(BF16)
+    grad = [dot(turned[:, pl.ds(k * frame, n)], diff) for k in range(3)]
     grad = jnp.concatenate(grad, 0) * scale_mid
     if reduce:
         mid_sum = Sum(sums[:12], gt_out, grad, d, me, members, others, spaces)
         mid_sum.first()
+        top_sum.third()
+        mid_sum.second()
         top_sum.fourth()
-        mid_sum.second()
         mid_sum.third()
         top_sum.finish()
         mid_sum.fourth()
@@ -400,8 +391,7 @@
     for u in peers:
         edge_copy(u, t).wait_send()
         feats_copy(u, t).wait_send()
-        for h in range(2):
-            teach_copy(u, t, h).wait_send()
+        teach_copy(u, t).wait_send()
         top_copy(u, t).wait_send()
         student_copy(u, t).wait_send()
 
@@ -457,7 +447,6 @@
         out_specs=(pl.BlockSpec(memory_space=pltpu.VMEM),) * 3,
         scratch_shapes=[
             pltpu.VMEM((rows, frames, wc, chan), BF16),
-            pltpu.VMEM((rows, frames, wc, chan), BF16),
             pltpu.VMEM((3, 3 * chan, chan), BF16),
             pltpu.VMEM(w_temporal.shape, BF16),
             pltpu.VMEM(w_down.shape, BF16),
@@ -471,16 +460,16 @@
             pltpu.VMEM((2, frames, 2 * rows, chan), BF16),
             pltpu.VMEM((rows + 2, frames * wc, 3 * chan), BF16),
             pltpu.VMEM((frames + 2, rows, wc, chan), BF16),
-            pltpu.VMEM((2, 3, chan, frames * rows * wc // 2), BF16),
+            pltpu.VMEM((chan, (frames + 2) * rows * wc), BF16),
             pltpu.VMEM((frames, rows, wc, chan), BF16),
             pltpu.VMEM((frames, half_rows, hc, width), BF16),
             pltpu.VMEM((2, frames * rows * wc, chan // 2), F32),
             pltpu.VMEM((frames, half_rows, hc, width), BF16),
-            dma((9,)),
+            dma((8,)),
             dma((4,)),
         ]
         + [dma((frames,))] * 4
-        + [dma((2 * frames,))] * 2
+        + [dma((frames,))] * 2
         + [dma((frames,))] * 4
         + [dma((4,)), dma((4,))]
         + (sum_scratch(grads[0], group, clips) + sum_scratch(grads[1], group, clips) if reduce else []),

time: 58.8 us -> 60.5 us (1.029)
  Pallas kernels: 58 us -> 59.7 us
    pallas_call x1, Pallas kernels: 56.2 us -> 58 us  [local(): pl.pallas_call(functools.partial(kernel, frames, spaces, clips, reduce, s...]
where the time goes in v8:
time: 60.5 us; the launch traced here: 60.4 us
  Pallas kernels  59.7 us (99%)
  between operations  0.64 us (1%)
    pallas_call x1, Pallas kernels, local(): pl.pallas_call(functools.partial(kernel, frames, spaces, clips, reduce, s...  58 us
    pallas_call x1, Pallas kernels, local(): pl.pallas_call(hand_over, out_shape=tuple((jax.ShapeDtypeStruct(x.shape,...  1.78 us

profile of v8, /device:TPU:0, one launch (start us, length us, event | category | flops | bytes accessed | tf_op | source)
XLA Modules:
  0.0 60.4 jit_solution(9834884090113713810)
XLA Ops:
  0.6 58.0 %shard_map.121 = (bf16[4,4,16,512]{3,2,1,0:T(8,128)(2,1)}, f32[96,256]{1,0:T(8,128)}, f32[64,512]{1,0:T(8,128)}) custom-call(bf16[8,4,32,256]{3,2,1,0:T(8,128)(2,1)} %bitcast.6, bf16[3,768,256]{2,1,0:T(8,128)(2,1)} %bitcast.5, bf16[768,256]{1,0:T(8,128)(2,1)} %w_tm.1, bf16[8,4,32,256]{3,2,1,0:T(8,128)(2,1)} %bitcast.7, bf16[2,2,256,512]{3,2,1,0:T(8,128)(2,1)} %w_dn.1, ...), custom_call_target="tpu_custom_call" | custom-call | tf_op jit(solution)/shard_map/pallas_call | solution.py:439
  58.6 1.8 %shard_map.122 = (bf16[4,4,16,512]{3,2,1,0:T(8,128)(2,1)}, f32[96,256]{1,0:T(8,128)}, f32[64,512]{1,0:T(8,128)}) custom-call(bf16[4,4,16,512]{3,2,1,0:T(8,128)(2,1)} %get-tuple-element.9.refs_0_, f32[96,256]{1,0:T(8,128)} %get-tuple-element.10.refs_1_, f32[64,512]{1,0:T(8,128)} %get-tuple-element.11.refs_2_), custom_call_target="tpu_custom_call" | custom-call | tf_op jit(solution)/shard_map/pallas_call | solution.py:492

commit v9 on v8

--- a/solution.py
+++ b/solution.py
@@ -363,6 +363,7 @@
         turned[:, pl.ds((f + 2) * frame, frame)] = spat[f + 2].reshape(frame, chan).T
     if reduce:
         top_sum.second()
+        top_sum.third()
     own[1].wait()
     for f in peers:
         teach_copy(f, f).wait_recv()
@@ -375,7 +376,6 @@
     if reduce:
         mid_sum = Sum(sums[:12], gt_out, grad, d, me, members, others, spaces)
         mid_sum.first()
-        top_sum.third()
         mid_sum.second()
         top_sum.fourth()
         mid_sum.third()

time: 60.5 us -> 55.7 us (0.921)
  Pallas kernels: 59.7 us -> 54.9 us
    pallas_call x1, Pallas kernels: 58 us -> 53.1 us  [local(): pl.pallas_call(functools.partial(kernel, frames, spaces, clips, reduce, s...]
where the time goes in v9:
time: 55.7 us; the launch traced here: 55.5 us
  Pallas kernels  54.9 us (99%)
  between operations  0.64 us (1%)
    pallas_call x1, Pallas kernels, local(): pl.pallas_call(functools.partial(kernel, frames, spaces, clips, reduce, s...  53.1 us
    pallas_call x1, Pallas kernels, local(): pl.pallas_call(hand_over, out_shape=tuple((jax.ShapeDtypeStruct(x.shape,...  1.78 us

profile of v9, /device:TPU:0, one launch (start us, length us, event | category | flops | bytes accessed | tf_op | source)
XLA Modules:
  0.0 55.5 jit_solution(3466684346617006677)
XLA Ops:
  0.6 53.1 %shard_map.121 = (bf16[4,4,16,512]{3,2,1,0:T(8,128)(2,1)}, f32[96,256]{1,0:T(8,128)}, f32[64,512]{1,0:T(8,128)}) custom-call(bf16[8,4,32,256]{3,2,1,0:T(8,128)(2,1)} %bitcast.6, bf16[3,768,256]{2,1,0:T(8,128)(2,1)} %bitcast.5, bf16[768,256]{1,0:T(8,128)(2,1)} %w_tm.1, bf16[8,4,32,256]{3,2,1,0:T(8,128)(2,1)} %bitcast.7, bf16[2,2,256,512]{3,2,1,0:T(8,128)(2,1)} %w_dn.1, ...), custom_call_target="tpu_custom_call" | custom-call | tf_op jit(solution)/shard_map/pallas_call | solution.py:439
  53.8 1.8 %shard_map.122 = (bf16[4,4,16,512]{3,2,1,0:T(8,128)(2,1)}, f32[96,256]{1,0:T(8,128)}, f32[64,512]{1,0:T(8,128)}) custom-call(bf16[4,4,16,512]{3,2,1,0:T(8,128)(2,1)} %get-tuple-element.9.refs_0_, f32[96,256]{1,0:T(8,128)} %get-tuple-element.10.refs_1_, f32[64,512]{1,0:T(8,128)} %get-tuple-element.11.refs_2_), custom_call_target="tpu_custom_call" | custom-call | tf_op jit(solution)/shard_map/pallas_call | solution.py:492
